TPU v7x, 32 devices: a whole 2x2x4 slice. The times are simulated.
32 devices in a mesh: groups: 2 (over x), shot: 2 (over core), space: 8 (over z, y).
Axes of the slice: x: 2, y: 2, z: 4, core: 2. Of those that a mesh axis runs over, the one named last changes fastest.
Arguments:
- coef: float32 [256, 128, 256], P(('groups', 'space')), parts along dimension 0, may hold values from 0.05 to 0.19
- fwd_prev: float32 [4, 128, 128, 256], P(('groups', 'shot'), 'space'), parts along dimension 0, may hold values from -1.2 to 1.2
- fwd_now: float32 [4, 128, 128, 256], P(('groups', 'shot'), 'space'), parts along dimension 0, may hold values from -1.2 to 1.2
- adj_next: float32 [4, 128, 128, 256], P(('groups', 'shot'), 'space'), parts along dimension 0, may hold values from -1.2 to 1.2
- adj_after: float32 [4, 128, 128, 256], P(('groups', 'shot'), 'space'), parts along dimension 0, may hold values from -1.2 to 1.2
- encode: float32 [4, 64], P(('groups', 'shot')), parts along dimension 0, may hold values from -4 to 4
- wavelet: float32 [20, 64], P('groups'), parts along dimension 0, may hold values from -4 to 4
- shot_cells: int32 [128], P('groups'), parts along dimension 0, may hold values from 0 to 4194303
- rec_cells: int32 [2048], P('groups'), parts along dimension 0, may hold values from 0 to 4194303
- records: float32 [4, 10, 1024], P(('groups', 'shot')), parts along dimension 0, may hold values from -1.2 to 1.2
Outputs:
- gradient: float32 [256, 128, 256], P(('groups', 'space'), 'shot'), parts along dimension 0
There are 2 independent parts, one for each index of `groups`. A program takes and returns all parts, laid end to end along the dimension named above; each array names one. Nothing has to cross between parts.
All inputs are finite; a program needn't handle non-finite values.
Results may differ from a plain program's by a relative error of at most 0.0001.
Values sent between devices are 32-bit elements; how exact they have to be, the bound alone decides.
A program may use at most 128 MiB of HBM per device.

v0:
```python
import jax
import jax.numpy as jnp
from jax import lax
from jax.sharding import PartitionSpec as P

stencil_weights = (-205.0 / 72.0, 8.0 / 5.0, -1.0 / 5.0, 8.0 / 315.0, -1.0 / 560.0)


def with_halo(block, sides, width):
    for axis, dim in sides:
        count = lax.axis_size(axis)
        forward = [(i, i + 1) for i in range(count - 1)]
        backward = [(target, source) for source, target in forward]
        low = lax.ppermute(
            lax.slice_in_dim(block, block.shape[dim] - width, None, axis=dim), axis, forward
        )
        high = lax.ppermute(lax.slice_in_dim(block, 0, width, axis=dim), axis, backward)
        block = jnp.concatenate([low, block, high], axis=dim)
    return block


def laplace(extended):
    breadth = extended.shape[-3] - 8
    center = extended[..., 4 : 4 + breadth, :, :]
    across = center.shape[-2]
    downward = center.shape[-1]
    leading = [(0, 0)] * (center.ndim - 2)
    padded = jnp.pad(center, leading + [(4, 4), (4, 4)])
    summed = 3.0 * stencil_weights[0] * center
    for offset in range(1, 5):
        along_x = (
            extended[..., 4 + offset : 4 + offset + breadth, :, :]
            + extended[..., 4 - offset : 4 - offset + breadth, :, :]
        )
        along_y = (
            padded[..., 4 + offset : 4 + offset + across, 4 : 4 + downward]
            + padded[..., 4 - offset : 4 - offset + across, 4 : 4 + downward]
        )
        along_z = (
            padded[..., 4 : 4 + across, 4 + offset : 4 + offset + downward]
            + padded[..., 4 : 4 + across, 4 - offset : 4 - offset + downward]
        )
        summed = summed + stencil_weights[offset] * (along_x + along_y + along_z)
    return summed


def shards(
    coef, fwd_prev, fwd_now, adj_next, adj_after, encode, wavelet, shot_cells, rec_cells, records
):
    supers = fwd_now.shape[0]
    plane = coef.shape[1] * coef.shape[2]
    anchor = lax.axis_index("space") * coef.shape[0]
    observed_all = jnp.moveaxis(records, 1, 0)

    def inject(field, amounts, cells, start):
        count = field.shape[1] * plane
        local_index = cells - start * plane
        inside = (local_index >= 0) & (local_index < count)
        target = jnp.where(inside, local_index, count)
        flat_field = field.reshape(supers, -1).at[:, target].add(amounts, mode="drop")
        return flat_field.reshape(field.shape)

    def sample(field, observed):
        count = field.shape[1] * plane
        local_index = rec_cells - anchor * plane
        inside = (local_index >= 0) & (local_index < count)
        picked = field.reshape(supers, -1)[:, jnp.where(inside, local_index, 0)]
        return jnp.where(inside[None, :], picked - observed, 0.0)

    def forward(carry, inputs):
        earlier, current = carry
        wave_row, observed = inputs
        extended = with_halo(current, (("space", 1),), 4)
        laplacian = laplace(extended)
        updated = 2.0 * current - earlier + coef * laplacian
        updated = inject(updated, encode * wave_row[None, :], shot_cells, anchor)
        return ((current, updated), (laplacian, sample(updated, observed)))

    _, (history, misfits) = lax.scan(forward, (fwd_prev, fwd_now), (wavelet, observed_all))

    def backward(carry, inputs):
        later, latest, gradient = carry
        laplacian, residue = inputs
        extended = with_halo(coef * later, (("space", 1),), 4)
        adjoint = 2.0 * later - latest + laplace(extended)
        adjoint = inject(adjoint, residue, rec_cells, anchor)
        gradient = gradient + jnp.sum(adjoint * laplacian, axis=0)
        return ((adjoint, later, gradient), None)

    start_gradient = jnp.zeros(coef.shape, jnp.float32)
    (_, _, gradient), _ = lax.scan(
        backward, (adj_next, adj_after, start_gradient), (history, misfits), reverse=True
    )
    return lax.psum_scatter(gradient, "shot", scatter_dimension=1, tiled=True)


def solution(mesh):
    placed = (
        P(("groups", "space"), None, None),
        P(("groups", "shot"), "space", None, None),
        P(("groups", "shot"), "space", None, None),
        P(("groups", "shot"), "space", None, None),
        P(("groups", "shot"), "space", None, None),
        P(("groups", "shot"), None),
        P("groups", None),
        P("groups"),
        P("groups"),
        P(("groups", "shot"), None, None),
    )
    return jax.shard_map(
        shards,
        mesh=mesh,
        in_specs=placed,
        out_specs=P(("groups", "space"), "shot", None),
        check_vma=False,
    )
```

profile of v0, /device:TPU:1, one launch (start us, length us, event | category | flops | bytes accessed | tf_op | source)
XLA Modules:
  0.0 1327.1 jit_solution(4568837034979697895)
XLA Ops:
  15.9 488.7 %while.37 = (s32[]{:T(128)}, f32[1,16,128,256]{3,2,1,0:T(8,128)}, f32[1,16,128,256]{3,2,1,0:T(8,128)S(1)}, f32[10,1,16,128,256]{4,3,2,1,0:T(8,128)}, f32[10,1,10...) while((s32[]{:T(128)}, f32[1,16,128,256]{3,2,1,0:T(8,128)}, ...), condition=%wide.region_2.3_spmd, body=%wide.region_0.2_spmd.sunk | while | flops 17316480 | bytes 86037040 | solution.py:79
  23.1 20.0 %collective-permute-done = f32[1,4,128,256]{3,2,1,0:T(8,128)S(1)} collective-permute-done((f32[1,4,128,256]{3,2,1,0:T(8,128)}, f32[1,4,128,256]{3,2,1,0:T(8,128)S(1)}, u32[]{:S(2)}, u32[]{:S(2)}) %collective-permute-start) | collective-permute-done | bytes 524320 | tf_op jit(solution)/shard_map/while/body/eval_jaxpr/ppermute | solution.py:14
  55.5 6.1 gather_fusion
  71.5 19.1 %collective-permute-done = f32[1,4,128,256]{3,2,1,0:T(8,128)S(1)} collective-permute-done((f32[1,4,128,256]{3,2,1,0:T(8,128)}, f32[1,4,128,256]{3,2,1,0:T(8,128)S(1)}, u32[]{:S(2)}, u32[]{:S(2)}) %collective-permute-start) | collective-permute-done | bytes 524320 | tf_op jit(solution)/shard_map/while/body/eval_jaxpr/ppermute | solution.py:14
  103.0 6.1 gather_fusion
  119.0 6.8 collective-permute-done
  126.3 9.2 collective-permute-done.1
  157.2 6.2 collective-permute-start
  172.1 13.2 collective-permute-done.1
  197.2 6.1 gather_fusion
  213.2 7.1 collective-permute-done
  220.9 14.3 %collective-permute-done.1 = f32[1,4,128,256]{3,2,1,0:T(8,128)S(1)} collective-permute-done((f32[1,4,128,256]{3,2,1,0:T(8,128)}, f32[1,4,128,256]{3,2,1,0:T(8,128)S(1)}, u32[]{:S(2)}, u32[]{:S(2)}) %collective-permute-start.1) | collective-permute-done | bytes 524320 | tf_op jit(solution)/shard_map/while/body/eval_jaxpr/ppermute | solution.py:17
  262.9 7.8 collective-permute-done
  271.2 13.8 %collective-permute-done.1 = f32[1,4,128,256]{3,2,1,0:T(8,128)S(1)} collective-permute-done((f32[1,4,128,256]{3,2,1,0:T(8,128)}, f32[1,4,128,256]{3,2,1,0:T(8,128)S(1)}, u32[]{:S(2)}, u32[]{:S(2)}) %collective-permute-start.1) | collective-permute-done | bytes 524320 | tf_op jit(solution)/shard_map/while/body/eval_jaxpr/ppermute | solution.py:17
  312.7 7.8 collective-permute-done
  321.0 13.8 %collective-permute-done.1 = f32[1,4,128,256]{3,2,1,0:T(8,128)S(1)} collective-permute-done((f32[1,4,128,256]{3,2,1,0:T(8,128)}, f32[1,4,128,256]{3,2,1,0:T(8,128)S(1)}, u32[]{:S(2)}, u32[]{:S(2)}) %collective-permute-start.1) | collective-permute-done | bytes 524320 | tf_op jit(solution)/shard_map/while/body/eval_jaxpr/ppermute | solution.py:17
  362.5 7.8 collective-permute-done
  370.8 13.8 %collective-permute-done.1 = f32[1,4,128,256]{3,2,1,0:T(8,128)S(1)} collective-permute-done((f32[1,4,128,256]{3,2,1,0:T(8,128)}, f32[1,4,128,256]{3,2,1,0:T(8,128)S(1)}, u32[]{:S(2)}, u32[]{:S(2)}) %collective-permute-start.1) | collective-permute-done | bytes 524320 | tf_op jit(solution)/shard_map/while/body/eval_jaxpr/ppermute | solution.py:17
  412.3 7.8 collective-permute-done
  420.6 13.8 %collective-permute-done.1 = f32[1,4,128,256]{3,2,1,0:T(8,128)S(1)} collective-permute-done((f32[1,4,128,256]{3,2,1,0:T(8,128)}, f32[1,4,128,256]{3,2,1,0:T(8,128)S(1)}, u32[]{:S(2)}, u32[]{:S(2)}) %collective-permute-start.1) | collective-permute-done | bytes 524320 | tf_op jit(solution)/shard_map/while/body/eval_jaxpr/ppermute | solution.py:17
  462.1 7.8 collective-permute-done
  470.4 13.8 %collective-permute-done.1 = f32[1,4,128,256]{3,2,1,0:T(8,128)S(1)} collective-permute-done((f32[1,4,128,256]{3,2,1,0:T(8,128)}, f32[1,4,128,256]{3,2,1,0:T(8,128)S(1)}, u32[]{:S(2)}, u32[]{:S(2)}) %collective-permute-start.1) | collective-permute-done | bytes 524320 | tf_op jit(solution)/shard_map/while/body/eval_jaxpr/ppermute | solution.py:17
  504.7 795.3 %while.38 = (s32[]{:T(128)}, f32[1,16,128,256]{3,2,1,0:T(8,128)}, f32[1,16,128,256]{3,2,1,0:T(8,128)}, f32[16,128,256]{2,1,0:T(8,128)}, f32[16,128,256]{2,1,0:T(...) while((s32[]{:T(128)}, f32[1,16,128,256]{3,2,1,0:T(8,128)}, ...), condition=%wide.region_5.6_spmd.clone, body=%wide.region_3.5_spmd.clone.sunk | while | flops 23077888 | bytes 64004380 | solution.py:91
  515.0 8.5 collective-permute-done.2
  523.5 14.3 %collective-permute-done.3 = f32[1,4,128,256]{3,2,1,0:T(8,128)S(1)} collective-permute-done((f32[1,4,128,256]{3,2,1,0:T(8,128)}, f32[1,4,128,256]{3,2,1,0:T(8,128)S(1)}, u32[]{:S(2)}, u32[]{:S(2)}) %collective-permute-start.3) | collective-permute-done | bytes 524320 | tf_op jit(solution)/shard_map/while/body/eval_jaxpr/ppermute | solution.py:17
  537.8 29.2 %fusion.82 = f32[1,16,128,256]{3,2,1,0:T(8,128)S(1)} fusion(f32[1,16,128,256]{3,2,1,0:T(8,128)} %copy-done.3, f32[1,4,128,256]{3,2,1,0:T(8,128)S(1)} %collective-permute-done.2, f32[1,4,128,256]{3,2,1,0:T(8,128)S(1)} %collective-permute-done.3, f32[1,16,128,256]{3,2,1,0:T(8,128)} %get-tuple-element.625, f32[1,16,128,256]{3,2,1,0:T(8,128)S(1)} %copy-done.2), kind=kLoop, calls=%fused_computation.102.clone.1 | loop fusion | flops 20971520 | bytes 9437184 | tf_op jit(solution)/shard_map/while/body/eval_jaxpr/add | solution.py:85
  569.5 6.8 scatter_fusion.1
  594.0 8.5 collective-permute-done.2
  602.5 14.3 %collective-permute-done.3 = f32[1,4,128,256]{3,2,1,0:T(8,128)S(1)} collective-permute-done((f32[1,4,128,256]{3,2,1,0:T(8,128)}, f32[1,4,128,256]{3,2,1,0:T(8,128)S(1)}, u32[]{:S(2)}, u32[]{:S(2)}) %collective-permute-start.3) | collective-permute-done | bytes 524320 | tf_op jit(solution)/shard_map/while/body/eval_jaxpr/ppermute | solution.py:17
  616.8 29.2 %fusion.82 = f32[1,16,128,256]{3,2,1,0:T(8,128)S(1)} fusion(f32[1,16,128,256]{3,2,1,0:T(8,128)} %copy-done.3, f32[1,4,128,256]{3,2,1,0:T(8,128)S(1)} %collective-permute-done.2, f32[1,4,128,256]{3,2,1,0:T(8,128)S(1)} %collective-permute-done.3, f32[1,16,128,256]{3,2,1,0:T(8,128)} %get-tuple-element.625, f32[1,16,128,256]{3,2,1,0:T(8,128)S(1)} %copy-done.2), kind=kLoop, calls=%fused_computation.102.clone.1 | loop fusion | flops 20971520 | bytes 9437184 | tf_op jit(solution)/shard_map/while/body/eval_jaxpr/add | solution.py:85
  648.4 6.8 scatter_fusion.1
  673.6 8.5 collective-permute-done.2
  682.1 14.3 %collective-permute-done.3 = f32[1,4,128,256]{3,2,1,0:T(8,128)S(1)} collective-permute-done((f32[1,4,128,256]{3,2,1,0:T(8,128)}, f32[1,4,128,256]{3,2,1,0:T(8,128)S(1)}, u32[]{:S(2)}, u32[]{:S(2)}) %collective-permute-start.3) | collective-permute-done | bytes 524320 | tf_op jit(solution)/shard_map/while/body/eval_jaxpr/ppermute | solution.py:17
  696.4 29.2 %fusion.82 = f32[1,16,128,256]{3,2,1,0:T(8,128)S(1)} fusion(f32[1,16,128,256]{3,2,1,0:T(8,128)} %copy-done.3, f32[1,4,128,256]{3,2,1,0:T(8,128)S(1)} %collective-permute-done.2, f32[1,4,128,256]{3,2,1,0:T(8,128)S(1)} %collective-permute-done.3, f32[1,16,128,256]{3,2,1,0:T(8,128)} %get-tuple-element.625, f32[1,16,128,256]{3,2,1,0:T(8,128)S(1)} %copy-done.2), kind=kLoop, calls=%fused_computation.102.clone.1 | loop fusion | flops 20971520 | bytes 9437184 | tf_op jit(solution)/shard_map/while/body/eval_jaxpr/add | solution.py:85
  728.0 6.8 scatter_fusion.1
  753.2 8.5 collective-permute-done.2
  761.7 14.3 %collective-permute-done.3 = f32[1,4,128,256]{3,2,1,0:T(8,128)S(1)} collective-permute-done((f32[1,4,128,256]{3,2,1,0:T(8,128)}, f32[1,4,128,256]{3,2,1,0:T(8,128)S(1)}, u32[]{:S(2)}, u32[]{:S(2)}) %collective-permute-start.3) | collective-permute-done | bytes 524320 | tf_op jit(solution)/shard_map/while/body/eval_jaxpr/ppermute | solution.py:17
  775.9 29.2 %fusion.82 = f32[1,16,128,256]{3,2,1,0:T(8,128)S(1)} fusion(f32[1,16,128,256]{3,2,1,0:T(8,128)} %copy-done.3, f32[1,4,128,256]{3,2,1,0:T(8,128)S(1)} %collective-permute-done.2, f32[1,4,128,256]{3,2,1,0:T(8,128)S(1)} %collective-permute-done.3, f32[1,16,128,256]{3,2,1,0:T(8,128)} %get-tuple-element.625, f32[1,16,128,256]{3,2,1,0:T(8,128)S(1)} %copy-done.2), kind=kLoop, calls=%fused_computation.102.clone.1 | loop fusion | flops 20971520 | bytes 9437184 | tf_op jit(solution)/shard_map/while/body/eval_jaxpr/add | solution.py:85
  807.6 6.8 scatter_fusion.1
  832.8 8.5 collective-permute-done.2
  841.3 14.3 %collective-permute-done.3 = f32[1,4,128,256]{3,2,1,0:T(8,128)S(1)} collective-permute-done((f32[1,4,128,256]{3,2,1,0:T(8,128)}, f32[1,4,128,256]{3,2,1,0:T(8,128)S(1)}, u32[]{:S(2)}, u32[]{:S(2)}) %collective-permute-start.3) | collective-permute-done | bytes 524320 | tf_op jit(solution)/shard_map/while/body/eval_jaxpr/ppermute | solution.py:17
  855.5 29.2 %fusion.82 = f32[1,16,128,256]{3,2,1,0:T(8,128)S(1)} fusion(f32[1,16,128,256]{3,2,1,0:T(8,128)} %copy-done.3, f32[1,4,128,256]{3,2,1,0:T(8,128)S(1)} %collective-permute-done.2, f32[1,4,128,256]{3,2,1,0:T(8,128)S(1)} %collective-permute-done.3, f32[1,16,128,256]{3,2,1,0:T(8,128)} %get-tuple-element.625, f32[1,16,128,256]{3,2,1,0:T(8,128)S(1)} %copy-done.2), kind=kLoop, calls=%fused_computation.102.clone.1 | loop fusion | flops 20971520 | bytes 9437184 | tf_op jit(solution)/shard_map/while/body/eval_jaxpr/add | solution.py:85
  887.2 6.8 scatter_fusion.1
  912.4 8.5 collective-permute-done.2
  920.8 14.3 %collective-permute-done.3 = f32[1,4,128,256]{3,2,1,0:T(8,128)S(1)} collective-permute-done((f32[1,4,128,256]{3,2,1,0:T(8,128)}, f32[1,4,128,256]{3,2,1,0:T(8,128)S(1)}, u32[]{:S(2)}, u32[]{:S(2)}) %collective-permute-start.3) | collective-permute-done | bytes 524320 | tf_op jit(solution)/shard_map/while/body/eval_jaxpr/ppermute | solution.py:17
  935.1 29.2 %fusion.82 = f32[1,16,128,256]{3,2,1,0:T(8,128)S(1)} fusion(f32[1,16,128,256]{3,2,1,0:T(8,128)} %copy-done.3, f32[1,4,128,256]{3,2,1,0:T(8,128)S(1)} %collective-permute-done.2, f32[1,4,128,256]{3,2,1,0:T(8,128)S(1)} %collective-permute-done.3, f32[1,16,128,256]{3,2,1,0:T(8,128)} %get-tuple-element.625, f32[1,16,128,256]{3,2,1,0:T(8,128)S(1)} %copy-done.2), kind=kLoop, calls=%fused_computation.102.clone.1 | loop fusion | flops 20971520 | bytes 9437184 | tf_op jit(solution)/shard_map/while/body/eval_jaxpr/add | solution.py:85
  966.8 6.8 scatter_fusion.1
  992.0 8.5 collective-permute-done.2
  1000.4 14.3 %collective-permute-done.3 = f32[1,4,128,256]{3,2,1,0:T(8,128)S(1)} collective-permute-done((f32[1,4,128,256]{3,2,1,0:T(8,128)}, f32[1,4,128,256]{3,2,1,0:T(8,128)S(1)}, u32[]{:S(2)}, u32[]{:S(2)}) %collective-permute-start.3) | collective-permute-done | bytes 524320 | tf_op jit(solution)/shard_map/while/body/eval_jaxpr/ppermute | solution.py:17
  1014.7 29.2 %fusion.82 = f32[1,16,128,256]{3,2,1,0:T(8,128)S(1)} fusion(f32[1,16,128,256]{3,2,1,0:T(8,128)} %copy-done.3, f32[1,4,128,256]{3,2,1,0:T(8,128)S(1)} %collective-permute-done.2, f32[1,4,128,256]{3,2,1,0:T(8,128)S(1)} %collective-permute-done.3, f32[1,16,128,256]{3,2,1,0:T(8,128)} %get-tuple-element.625, f32[1,16,128,256]{3,2,1,0:T(8,128)S(1)} %copy-done.2), kind=kLoop, calls=%fused_computation.102.clone.1 | loop fusion | flops 20971520 | bytes 9437184 | tf_op jit(solution)/shard_map/while/body/eval_jaxpr/add | solution.py:85
  1046.4 6.8 scatter_fusion.1
  1071.6 8.5 collective-permute-done.2
  1080.0 14.3 %collective-permute-done.3 = f32[1,4,128,256]{3,2,1,0:T(8,128)S(1)} collective-permute-done((f32[1,4,128,256]{3,2,1,0:T(8,128)}, f32[1,4,128,256]{3,2,1,0:T(8,128)S(1)}, u32[]{:S(2)}, u32[]{:S(2)}) %collective-permute-start.3) | collective-permute-done | bytes 524320 | tf_op jit(solution)/shard_map/while/body/eval_jaxpr/ppermute | solution.py:17
  1094.3 29.2 %fusion.82 = f32[1,16,128,256]{3,2,1,0:T(8,128)S(1)} fusion(f32[1,16,128,256]{3,2,1,0:T(8,128)} %copy-done.3, f32[1,4,128,256]{3,2,1,0:T(8,128)S(1)} %collective-permute-done.2, f32[1,4,128,256]{3,2,1,0:T(8,128)S(1)} %collective-permute-done.3, f32[1,16,128,256]{3,2,1,0:T(8,128)} %get-tuple-element.625, f32[1,16,128,256]{3,2,1,0:T(8,128)S(1)} %copy-done.2), kind=kLoop, calls=%fused_computation.102.clone.1 | loop fusion | flops 20971520 | bytes 9437184 | tf_op jit(solution)/shard_map/while/body/eval_jaxpr/add | solution.py:85
  1126.0 6.8 scatter_fusion.1
  1151.1 8.5 collective-permute-done.2
  1159.6 14.3 %collective-permute-done.3 = f32[1,4,128,256]{3,2,1,0:T(8,128)S(1)} collective-permute-done((f32[1,4,128,256]{3,2,1,0:T(8,128)}, f32[1,4,128,256]{3,2,1,0:T(8,128)S(1)}, u32[]{:S(2)}, u32[]{:S(2)}) %collective-permute-start.3) | collective-permute-done | bytes 524320 | tf_op jit(solution)/shard_map/while/body/eval_jaxpr/ppermute | solution.py:17
  1173.9 29.2 %fusion.82 = f32[1,16,128,256]{3,2,1,0:T(8,128)S(1)} fusion(f32[1,16,128,256]{3,2,1,0:T(8,128)} %copy-done.3, f32[1,4,128,256]{3,2,1,0:T(8,128)S(1)} %collective-permute-done.2, f32[1,4,128,256]{3,2,1,0:T(8,128)S(1)} %collective-permute-done.3, f32[1,16,128,256]{3,2,1,0:T(8,128)} %get-tuple-element.625, f32[1,16,128,256]{3,2,1,0:T(8,128)S(1)} %copy-done.2), kind=kLoop, calls=%fused_computation.102.clone.1 | loop fusion | flops 20971520 | bytes 9437184 | tf_op jit(solution)/shard_map/while/body/eval_jaxpr/add | solution.py:85
  1205.6 6.8 scatter_fusion.1
  1230.7 8.5 collective-permute-done.2
  1239.2 14.3 %collective-permute-done.3 = f32[1,4,128,256]{3,2,1,0:T(8,128)S(1)} collective-permute-done((f32[1,4,128,256]{3,2,1,0:T(8,128)}, f32[1,4,128,256]{3,2,1,0:T(8,128)S(1)}, u32[]{:S(2)}, u32[]{:S(2)}) %collective-permute-start.3) | collective-permute-done | bytes 524320 | tf_op jit(solution)/shard_map/while/body/eval_jaxpr/ppermute | solution.py:17
  1253.5 29.2 %fusion.82 = f32[1,16,128,256]{3,2,1,0:T(8,128)S(1)} fusion(f32[1,16,128,256]{3,2,1,0:T(8,128)} %copy-done.3, f32[1,4,128,256]{3,2,1,0:T(8,128)S(1)} %collective-permute-done.2, f32[1,4,128,256]{3,2,1,0:T(8,128)S(1)} %collective-permute-done.3, f32[1,16,128,256]{3,2,1,0:T(8,128)} %get-tuple-element.625, f32[1,16,128,256]{3,2,1,0:T(8,128)S(1)} %copy-done.2), kind=kLoop, calls=%fused_computation.102.clone.1 | loop fusion | flops 20971520 | bytes 9437184 | tf_op jit(solution)/shard_map/while/body/eval_jaxpr/add | solution.py:85
  1285.2 6.8 scatter_fusion.1
  1300.0 20.3 %reduce-scatter.2.cloned.1.call-done = f32[16,64,256]{2,1,0:T(8,128)} async-done(((f32[16,128,256]{2,1,0:T(8,128)}), f32[16,64,256]{2,1,0:T(8,128)}) %reduce-scatter.2.cloned.1.call-update) | async-done | bytes 1048592 | tf_op jit(solution)/shard_map/reduce_scatter | solution.py:94
  (429 shorter events, 481.1 us)
Async XLA Ops:
  6.5 1313.8 %reduce-scatter.2.cloned.1.call-start = ((), (), s32[]{:S(2)}) async-start(), calls=%async_computation.1 | async-start | bytes 3145728 | tf_op jit(solution)/shard_map/reduce_scatter | solution.py:94
  17.1 26.1 %collective-permute-start = (f32[1,4,128,256]{3,2,1,0:T(8,128)}, f32[1,4,128,256]{3,2,1,0:T(8,128)S(1)}, u32[]{:S(2)}, u32[]{:S(2)}) collective-permute-start(f32[1,4,128,256]{3,2,1,0:T(8,128)} %get-tuple-element.553), channel_id=1, source_target_pairs={{0,1},{1,2},{2,3},{3,4},{4,5},{5,6},{6,7},{8,9},{9,10},{10,11},{11... | collective-permute-start | bytes 1572872 | tf_op jit(solution)/shard_map/while/body/eval_jaxpr/ppermute | solution.py:14
  21.1 22.6 %collective-permute-start.1 = (f32[1,4,128,256]{3,2,1,0:T(8,128)}, f32[1,4,128,256]{3,2,1,0:T(8,128)S(1)}, u32[]{:S(2)}, u32[]{:S(2)}) collective-permute-start(f32[1,4,128,256]{3,2,1,0:T(8,128)} %get-tuple-element.556), channel_id=1, source_target_pairs={{1,0},{2,1},{3,2},{4,3},{5,4},{6,5},{7,6},{9,8},{10,9},{11,10},{12... | collective-permute-start | bytes 1572872 | tf_op jit(solution)/shard_map/while/body/eval_jaxpr/ppermute | solution.py:17
  43.8 5.7 copy-start.4
  43.8 5.7 copy-start.5
  65.4 25.2 %collective-permute-start = (f32[1,4,128,256]{3,2,1,0:T(8,128)}, f32[1,4,128,256]{3,2,1,0:T(8,128)S(1)}, u32[]{:S(2)}, u32[]{:S(2)}) collective-permute-start(f32[1,4,128,256]{3,2,1,0:T(8,128)} %get-tuple-element.553), channel_id=1, source_target_pairs={{0,1},{1,2},{2,3},{3,4},{4,5},{5,6},{6,7},{8,9},{9,10},{10,11},{11... | collective-permute-start | bytes 1572872 | tf_op jit(solution)/shard_map/while/body/eval_jaxpr/ppermute | solution.py:14
  69.5 21.7 %collective-permute-start.1 = (f32[1,4,128,256]{3,2,1,0:T(8,128)}, f32[1,4,128,256]{3,2,1,0:T(8,128)S(1)}, u32[]{:S(2)}, u32[]{:S(2)}) collective-permute-start(f32[1,4,128,256]{3,2,1,0:T(8,128)} %get-tuple-element.556), channel_id=1, source_target_pairs={{1,0},{2,1},{3,2},{4,3},{5,4},{6,5},{7,6},{9,8},{10,9},{11,10},{12... | collective-permute-start | bytes 1572872 | tf_op jit(solution)/shard_map/while/body/eval_jaxpr/ppermute | solution.py:17
  91.2 5.7 copy-start.4
  112.9 12.9 collective-permute-start
  116.9 18.6 %collective-permute-start.1 = (f32[1,4,128,256]{3,2,1,0:T(8,128)}, f32[1,4,128,256]{3,2,1,0:T(8,128)S(1)}, u32[]{:S(2)}, u32[]{:S(2)}) collective-permute-start(f32[1,4,128,256]{3,2,1,0:T(8,128)} %get-tuple-element.556), channel_id=1, source_target_pairs={{1,0},{2,1},{3,2},{4,3},{5,4},{6,5},{7,6},{9,8},{10,9},{11,10},{12... | collective-permute-start | bytes 1572872 | tf_op jit(solution)/shard_map/while/body/eval_jaxpr/ppermute | solution.py:17
  135.6 5.7 copy-start.4
  135.6 5.7 copy-start.5
  157.2 14.3 %collective-permute-start = (f32[1,4,128,256]{3,2,1,0:T(8,128)}, f32[1,4,128,256]{3,2,1,0:T(8,128)S(1)}, u32[]{:S(2)}, u32[]{:S(2)}) collective-permute-start(f32[1,4,128,256]{3,2,1,0:T(8,128)} %get-tuple-element.553), channel_id=1, source_target_pairs={{0,1},{1,2},{2,3},{3,4},{4,5},{5,6},{6,7},{8,9},{9,10},{10,11},{11... | collective-permute-start | bytes 1572872 | tf_op jit(solution)/shard_map/while/body/eval_jaxpr/ppermute | solution.py:14
  163.5 21.9 %collective-permute-start.1 = (f32[1,4,128,256]{3,2,1,0:T(8,128)}, f32[1,4,128,256]{3,2,1,0:T(8,128)S(1)}, u32[]{:S(2)}, u32[]{:S(2)}) collective-permute-start(f32[1,4,128,256]{3,2,1,0:T(8,128)} %get-tuple-element.556), channel_id=1, source_target_pairs={{1,0},{2,1},{3,2},{4,3},{5,4},{6,5},{7,6},{9,8},{10,9},{11,10},{12... | collective-permute-start | bytes 1572872 | tf_op jit(solution)/shard_map/while/body/eval_jaxpr/ppermute | solution.py:17
  185.4 5.8 copy-start.4
  185.4 5.7 copy-start.5
  207.1 13.3 collective-permute-start
  211.1 24.0 %collective-permute-start.1 = (f32[1,4,128,256]{3,2,1,0:T(8,128)}, f32[1,4,128,256]{3,2,1,0:T(8,128)S(1)}, u32[]{:S(2)}, u32[]{:S(2)}) collective-permute-start(f32[1,4,128,256]{3,2,1,0:T(8,128)} %get-tuple-element.556), channel_id=1, source_target_pairs={{1,0},{2,1},{3,2},{4,3},{5,4},{6,5},{7,6},{9,8},{10,9},{11,10},{12... | collective-permute-start | bytes 1572872 | tf_op jit(solution)/shard_map/while/body/eval_jaxpr/ppermute | solution.py:17
  235.2 5.7 copy-start.4
  235.2 5.7 copy-start.5
  256.9 13.8 %collective-permute-start = (f32[1,4,128,256]{3,2,1,0:T(8,128)}, f32[1,4,128,256]{3,2,1,0:T(8,128)S(1)}, u32[]{:S(2)}, u32[]{:S(2)}) collective-permute-start(f32[1,4,128,256]{3,2,1,0:T(8,128)} %get-tuple-element.553), channel_id=1, source_target_pairs={{0,1},{1,2},{2,3},{3,4},{4,5},{5,6},{6,7},{8,9},{9,10},{10,11},{11... | collective-permute-start | bytes 1572872 | tf_op jit(solution)/shard_map/while/body/eval_jaxpr/ppermute | solution.py:14
  260.9 24.1 %collective-permute-start.1 = (f32[1,4,128,256]{3,2,1,0:T(8,128)}, f32[1,4,128,256]{3,2,1,0:T(8,128)S(1)}, u32[]{:S(2)}, u32[]{:S(2)}) collective-permute-start(f32[1,4,128,256]{3,2,1,0:T(8,128)} %get-tuple-element.556), channel_id=1, source_target_pairs={{1,0},{2,1},{3,2},{4,3},{5,4},{6,5},{7,6},{9,8},{10,9},{11,10},{12... | collective-permute-start | bytes 1572872 | tf_op jit(solution)/shard_map/while/body/eval_jaxpr/ppermute | solution.py:17
  306.7 13.8 %collective-permute-start = (f32[1,4,128,256]{3,2,1,0:T(8,128)}, f32[1,4,128,256]{3,2,1,0:T(8,128)S(1)}, u32[]{:S(2)}, u32[]{:S(2)}) collective-permute-start(f32[1,4,128,256]{3,2,1,0:T(8,128)} %get-tuple-element.553), channel_id=1, source_target_pairs={{0,1},{1,2},{2,3},{3,4},{4,5},{5,6},{6,7},{8,9},{9,10},{10,11},{11... | collective-permute-start | bytes 1572872 | tf_op jit(solution)/shard_map/while/body/eval_jaxpr/ppermute | solution.py:14
  310.6 24.1 %collective-permute-start.1 = (f32[1,4,128,256]{3,2,1,0:T(8,128)}, f32[1,4,128,256]{3,2,1,0:T(8,128)S(1)}, u32[]{:S(2)}, u32[]{:S(2)}) collective-permute-start(f32[1,4,128,256]{3,2,1,0:T(8,128)} %get-tuple-element.556), channel_id=1, source_target_pairs={{1,0},{2,1},{3,2},{4,3},{5,4},{6,5},{7,6},{9,8},{10,9},{11,10},{12... | collective-permute-start | bytes 1572872 | tf_op jit(solution)/shard_map/while/body/eval_jaxpr/ppermute | solution.py:17
  356.4 13.8 %collective-permute-start = (f32[1,4,128,256]{3,2,1,0:T(8,128)}, f32[1,4,128,256]{3,2,1,0:T(8,128)S(1)}, u32[]{:S(2)}, u32[]{:S(2)}) collective-permute-start(f32[1,4,128,256]{3,2,1,0:T(8,128)} %get-tuple-element.553), channel_id=1, source_target_pairs={{0,1},{1,2},{2,3},{3,4},{4,5},{5,6},{6,7},{8,9},{9,10},{10,11},{11... | collective-permute-start | bytes 1572872 | tf_op jit(solution)/shard_map/while/body/eval_jaxpr/ppermute | solution.py:14
  360.4 24.1 %collective-permute-start.1 = (f32[1,4,128,256]{3,2,1,0:T(8,128)}, f32[1,4,128,256]{3,2,1,0:T(8,128)S(1)}, u32[]{:S(2)}, u32[]{:S(2)}) collective-permute-start(f32[1,4,128,256]{3,2,1,0:T(8,128)} %get-tuple-element.556), channel_id=1, source_target_pairs={{1,0},{2,1},{3,2},{4,3},{5,4},{6,5},{7,6},{9,8},{10,9},{11,10},{12... | collective-permute-start | bytes 1572872 | tf_op jit(solution)/shard_map/while/body/eval_jaxpr/ppermute | solution.py:17
  384.5 5.7 copy-start.4
  384.6 5.7 copy-start.5
  406.2 13.8 %collective-permute-start = (f32[1,4,128,256]{3,2,1,0:T(8,128)}, f32[1,4,128,256]{3,2,1,0:T(8,128)S(1)}, u32[]{:S(2)}, u32[]{:S(2)}) collective-permute-start(f32[1,4,128,256]{3,2,1,0:T(8,128)} %get-tuple-element.553), channel_id=1, source_target_pairs={{0,1},{1,2},{2,3},{3,4},{4,5},{5,6},{6,7},{8,9},{9,10},{10,11},{11... | collective-permute-start | bytes 1572872 | tf_op jit(solution)/shard_map/while/body/eval_jaxpr/ppermute | solution.py:14
  410.2 24.1 %collective-permute-start.1 = (f32[1,4,128,256]{3,2,1,0:T(8,128)}, f32[1,4,128,256]{3,2,1,0:T(8,128)S(1)}, u32[]{:S(2)}, u32[]{:S(2)}) collective-permute-start(f32[1,4,128,256]{3,2,1,0:T(8,128)} %get-tuple-element.556), channel_id=1, source_target_pairs={{1,0},{2,1},{3,2},{4,3},{5,4},{6,5},{7,6},{9,8},{10,9},{11,10},{12... | collective-permute-start | bytes 1572872 | tf_op jit(solution)/shard_map/while/body/eval_jaxpr/ppermute | solution.py:17
  434.4 5.7 copy-start.4
  456.0 13.8 %collective-permute-start = (f32[1,4,128,256]{3,2,1,0:T(8,128)}, f32[1,4,128,256]{3,2,1,0:T(8,128)S(1)}, u32[]{:S(2)}, u32[]{:S(2)}) collective-permute-start(f32[1,4,128,256]{3,2,1,0:T(8,128)} %get-tuple-element.553), channel_id=1, source_target_pairs={{0,1},{1,2},{2,3},{3,4},{4,5},{5,6},{6,7},{8,9},{9,10},{10,11},{11... | collective-permute-start | bytes 1572872 | tf_op jit(solution)/shard_map/while/body/eval_jaxpr/ppermute | solution.py:14
  460.0 24.1 %collective-permute-start.1 = (f32[1,4,128,256]{3,2,1,0:T(8,128)}, f32[1,4,128,256]{3,2,1,0:T(8,128)S(1)}, u32[]{:S(2)}, u32[]{:S(2)}) collective-permute-start(f32[1,4,128,256]{3,2,1,0:T(8,128)} %get-tuple-element.556), channel_id=1, source_target_pairs={{1,0},{2,1},{3,2},{4,3},{5,4},{6,5},{7,6},{9,8},{10,9},{11,10},{12... | collective-permute-start | bytes 1572872 | tf_op jit(solution)/shard_map/while/body/eval_jaxpr/ppermute | solution.py:17
  484.1 5.7 copy-start.4
  508.6 29.2 %copy-start.2 = (f32[1,16,128,256]{3,2,1,0:T(8,128)S(1)}, f32[1,16,128,256]{3,2,1,0:T(8,128)}, u32[]{:S(2)}) copy-start(f32[1,16,128,256]{3,2,1,0:T(8,128)} %get-tuple-element.624) | copy-start | bytes 6291460 | tf_op jit(solution)/shard_map/while
  509.7 13.8 %collective-permute-start.2 = (f32[1,4,128,256]{3,2,1,0:T(8,128)}, f32[1,4,128,256]{3,2,1,0:T(8,128)S(1)}, u32[]{:S(2)}, u32[]{:S(2)}) collective-permute-start(f32[1,4,128,256]{3,2,1,0:T(8,128)} %get-tuple-element.570), channel_id=1, source_target_pairs={{0,1},{1,2},{2,3},{3,4},{4,5},{5,6},{6,7},{8,9},{9,10},{10,11},{11... | collective-permute-start | bytes 1572872 | tf_op jit(solution)/shard_map/while/body/eval_jaxpr/ppermute | solution.py:14
  513.7 24.1 %collective-permute-start.3 = (f32[1,4,128,256]{3,2,1,0:T(8,128)}, f32[1,4,128,256]{3,2,1,0:T(8,128)S(1)}, u32[]{:S(2)}, u32[]{:S(2)}) collective-permute-start(f32[1,4,128,256]{3,2,1,0:T(8,128)} %get-tuple-element.571), channel_id=1, source_target_pairs={{1,0},{2,1},{3,2},{4,3},{5,4},{6,5},{7,6},{9,8},{10,9},{11,10},{12... | collective-permute-start | bytes 1572872 | tf_op jit(solution)/shard_map/while/body/eval_jaxpr/ppermute | solution.py:17
  587.6 29.2 %copy-start.2 = (f32[1,16,128,256]{3,2,1,0:T(8,128)S(1)}, f32[1,16,128,256]{3,2,1,0:T(8,128)}, u32[]{:S(2)}) copy-start(f32[1,16,128,256]{3,2,1,0:T(8,128)} %get-tuple-element.624) | copy-start | bytes 6291460 | tf_op jit(solution)/shard_map/while
  588.7 13.8 %collective-permute-start.2 = (f32[1,4,128,256]{3,2,1,0:T(8,128)}, f32[1,4,128,256]{3,2,1,0:T(8,128)S(1)}, u32[]{:S(2)}, u32[]{:S(2)}) collective-permute-start(f32[1,4,128,256]{3,2,1,0:T(8,128)} %get-tuple-element.570), channel_id=1, source_target_pairs={{0,1},{1,2},{2,3},{3,4},{4,5},{5,6},{6,7},{8,9},{9,10},{10,11},{11... | collective-permute-start | bytes 1572872 | tf_op jit(solution)/shard_map/while/body/eval_jaxpr/ppermute | solution.py:14
  592.7 24.1 %collective-permute-start.3 = (f32[1,4,128,256]{3,2,1,0:T(8,128)}, f32[1,4,128,256]{3,2,1,0:T(8,128)S(1)}, u32[]{:S(2)}, u32[]{:S(2)}) collective-permute-start(f32[1,4,128,256]{3,2,1,0:T(8,128)} %get-tuple-element.571), channel_id=1, source_target_pairs={{1,0},{2,1},{3,2},{4,3},{5,4},{6,5},{7,6},{9,8},{10,9},{11,10},{12... | collective-permute-start | bytes 1572872 | tf_op jit(solution)/shard_map/while/body/eval_jaxpr/ppermute | solution.py:17
  667.1 29.2 %copy-start.2 = (f32[1,16,128,256]{3,2,1,0:T(8,128)S(1)}, f32[1,16,128,256]{3,2,1,0:T(8,128)}, u32[]{:S(2)}) copy-start(f32[1,16,128,256]{3,2,1,0:T(8,128)} %get-tuple-element.624) | copy-start | bytes 6291460 | tf_op jit(solution)/shard_map/while
  668.3 13.8 %collective-permute-start.2 = (f32[1,4,128,256]{3,2,1,0:T(8,128)}, f32[1,4,128,256]{3,2,1,0:T(8,128)S(1)}, u32[]{:S(2)}, u32[]{:S(2)}) collective-permute-start(f32[1,4,128,256]{3,2,1,0:T(8,128)} %get-tuple-element.570), channel_id=1, source_target_pairs={{0,1},{1,2},{2,3},{3,4},{4,5},{5,6},{6,7},{8,9},{9,10},{10,11},{11... | collective-permute-start | bytes 1572872 | tf_op jit(solution)/shard_map/while/body/eval_jaxpr/ppermute | solution.py:14
  672.2 24.1 %collective-permute-start.3 = (f32[1,4,128,256]{3,2,1,0:T(8,128)}, f32[1,4,128,256]{3,2,1,0:T(8,128)S(1)}, u32[]{:S(2)}, u32[]{:S(2)}) collective-permute-start(f32[1,4,128,256]{3,2,1,0:T(8,128)} %get-tuple-element.571), channel_id=1, source_target_pairs={{1,0},{2,1},{3,2},{4,3},{5,4},{6,5},{7,6},{9,8},{10,9},{11,10},{12... | collective-permute-start | bytes 1572872 | tf_op jit(solution)/shard_map/while/body/eval_jaxpr/ppermute | solution.py:17
  746.7 29.2 %copy-start.2 = (f32[1,16,128,256]{3,2,1,0:T(8,128)S(1)}, f32[1,16,128,256]{3,2,1,0:T(8,128)}, u32[]{:S(2)}) copy-start(f32[1,16,128,256]{3,2,1,0:T(8,128)} %get-tuple-element.624) | copy-start | bytes 6291460 | tf_op jit(solution)/shard_map/while
  747.9 13.8 %collective-permute-start.2 = (f32[1,4,128,256]{3,2,1,0:T(8,128)}, f32[1,4,128,256]{3,2,1,0:T(8,128)S(1)}, u32[]{:S(2)}, u32[]{:S(2)}) collective-permute-start(f32[1,4,128,256]{3,2,1,0:T(8,128)} %get-tuple-element.570), channel_id=1, source_target_pairs={{0,1},{1,2},{2,3},{3,4},{4,5},{5,6},{6,7},{8,9},{9,10},{10,11},{11... | collective-permute-start | bytes 1572872 | tf_op jit(solution)/shard_map/while/body/eval_jaxpr/ppermute | solution.py:14
  751.8 24.1 %collective-permute-start.3 = (f32[1,4,128,256]{3,2,1,0:T(8,128)}, f32[1,4,128,256]{3,2,1,0:T(8,128)S(1)}, u32[]{:S(2)}, u32[]{:S(2)}) collective-permute-start(f32[1,4,128,256]{3,2,1,0:T(8,128)} %get-tuple-element.571), channel_id=1, source_target_pairs={{1,0},{2,1},{3,2},{4,3},{5,4},{6,5},{7,6},{9,8},{10,9},{11,10},{12... | collective-permute-start | bytes 1572872 | tf_op jit(solution)/shard_map/while/body/eval_jaxpr/ppermute | solution.py:17
  826.3 29.2 %copy-start.2 = (f32[1,16,128,256]{3,2,1,0:T(8,128)S(1)}, f32[1,16,128,256]{3,2,1,0:T(8,128)}, u32[]{:S(2)}) copy-start(f32[1,16,128,256]{3,2,1,0:T(8,128)} %get-tuple-element.624) | copy-start | bytes 6291460 | tf_op jit(solution)/shard_map/while
  827.5 13.8 %collective-permute-start.2 = (f32[1,4,128,256]{3,2,1,0:T(8,128)}, f32[1,4,128,256]{3,2,1,0:T(8,128)S(1)}, u32[]{:S(2)}, u32[]{:S(2)}) collective-permute-start(f32[1,4,128,256]{3,2,1,0:T(8,128)} %get-tuple-element.570), channel_id=1, source_target_pairs={{0,1},{1,2},{2,3},{3,4},{4,5},{5,6},{6,7},{8,9},{9,10},{10,11},{11... | collective-permute-start | bytes 1572872 | tf_op jit(solution)/shard_map/while/body/eval_jaxpr/ppermute | solution.py:14
  831.4 24.1 %collective-permute-start.3 = (f32[1,4,128,256]{3,2,1,0:T(8,128)}, f32[1,4,128,256]{3,2,1,0:T(8,128)S(1)}, u32[]{:S(2)}, u32[]{:S(2)}) collective-permute-start(f32[1,4,128,256]{3,2,1,0:T(8,128)} %get-tuple-element.571), channel_id=1, source_target_pairs={{1,0},{2,1},{3,2},{4,3},{5,4},{6,5},{7,6},{9,8},{10,9},{11,10},{12... | collective-permute-start | bytes 1572872 | tf_op jit(solution)/shard_map/while/body/eval_jaxpr/ppermute | solution.py:17
  905.9 29.2 %copy-start.2 = (f32[1,16,128,256]{3,2,1,0:T(8,128)S(1)}, f32[1,16,128,256]{3,2,1,0:T(8,128)}, u32[]{:S(2)}) copy-start(f32[1,16,128,256]{3,2,1,0:T(8,128)} %get-tuple-element.624) | copy-start | bytes 6291460 | tf_op jit(solution)/shard_map/while
  907.1 13.8 %collective-permute-start.2 = (f32[1,4,128,256]{3,2,1,0:T(8,128)}, f32[1,4,128,256]{3,2,1,0:T(8,128)S(1)}, u32[]{:S(2)}, u32[]{:S(2)}) collective-permute-start(f32[1,4,128,256]{3,2,1,0:T(8,128)} %get-tuple-element.570), channel_id=1, source_target_pairs={{0,1},{1,2},{2,3},{3,4},{4,5},{5,6},{6,7},{8,9},{9,10},{10,11},{11... | collective-permute-start | bytes 1572872 | tf_op jit(solution)/shard_map/while/body/eval_jaxpr/ppermute | solution.py:14
  911.0 24.1 %collective-permute-start.3 = (f32[1,4,128,256]{3,2,1,0:T(8,128)}, f32[1,4,128,256]{3,2,1,0:T(8,128)S(1)}, u32[]{:S(2)}, u32[]{:S(2)}) collective-permute-start(f32[1,4,128,256]{3,2,1,0:T(8,128)} %get-tuple-element.571), channel_id=1, source_target_pairs={{1,0},{2,1},{3,2},{4,3},{5,4},{6,5},{7,6},{9,8},{10,9},{11,10},{12... | collective-permute-start | bytes 1572872 | tf_op jit(solution)/shard_map/while/body/eval_jaxpr/ppermute | solution.py:17
  985.5 29.2 %copy-start.2 = (f32[1,16,128,256]{3,2,1,0:T(8,128)S(1)}, f32[1,16,128,256]{3,2,1,0:T(8,128)}, u32[]{:S(2)}) copy-start(f32[1,16,128,256]{3,2,1,0:T(8,128)} %get-tuple-element.624) | copy-start | bytes 6291460 | tf_op jit(solution)/shard_map/while
  986.6 13.8 %collective-permute-start.2 = (f32[1,4,128,256]{3,2,1,0:T(8,128)}, f32[1,4,128,256]{3,2,1,0:T(8,128)S(1)}, u32[]{:S(2)}, u32[]{:S(2)}) collective-permute-start(f32[1,4,128,256]{3,2,1,0:T(8,128)} %get-tuple-element.570), channel_id=1, source_target_pairs={{0,1},{1,2},{2,3},{3,4},{4,5},{5,6},{6,7},{8,9},{9,10},{10,11},{11... | collective-permute-start | bytes 1572872 | tf_op jit(solution)/shard_map/while/body/eval_jaxpr/ppermute | solution.py:14
  990.6 24.1 %collective-permute-start.3 = (f32[1,4,128,256]{3,2,1,0:T(8,128)}, f32[1,4,128,256]{3,2,1,0:T(8,128)S(1)}, u32[]{:S(2)}, u32[]{:S(2)}) collective-permute-start(f32[1,4,128,256]{3,2,1,0:T(8,128)} %get-tuple-element.571), channel_id=1, source_target_pairs={{1,0},{2,1},{3,2},{4,3},{5,4},{6,5},{7,6},{9,8},{10,9},{11,10},{12... | collective-permute-start | bytes 1572872 | tf_op jit(solution)/shard_map/while/body/eval_jaxpr/ppermute | solution.py:17
  1065.1 29.2 %copy-start.2 = (f32[1,16,128,256]{3,2,1,0:T(8,128)S(1)}, f32[1,16,128,256]{3,2,1,0:T(8,128)}, u32[]{:S(2)}) copy-start(f32[1,16,128,256]{3,2,1,0:T(8,128)} %get-tuple-element.624) | copy-start | bytes 6291460 | tf_op jit(solution)/shard_map/while
  1066.2 13.8 %collective-permute-start.2 = (f32[1,4,128,256]{3,2,1,0:T(8,128)}, f32[1,4,128,256]{3,2,1,0:T(8,128)S(1)}, u32[]{:S(2)}, u32[]{:S(2)}) collective-permute-start(f32[1,4,128,256]{3,2,1,0:T(8,128)} %get-tuple-element.570), channel_id=1, source_target_pairs={{0,1},{1,2},{2,3},{3,4},{4,5},{5,6},{6,7},{8,9},{9,10},{10,11},{11... | collective-permute-start | bytes 1572872 | tf_op jit(solution)/shard_map/while/body/eval_jaxpr/ppermute | solution.py:14
  1070.2 24.1 %collective-permute-start.3 = (f32[1,4,128,256]{3,2,1,0:T(8,128)}, f32[1,4,128,256]{3,2,1,0:T(8,128)S(1)}, u32[]{:S(2)}, u32[]{:S(2)}) collective-permute-start(f32[1,4,128,256]{3,2,1,0:T(8,128)} %get-tuple-element.571), channel_id=1, source_target_pairs={{1,0},{2,1},{3,2},{4,3},{5,4},{6,5},{7,6},{9,8},{10,9},{11,10},{12... | collective-permute-start | bytes 1572872 | tf_op jit(solution)/shard_map/while/body/eval_jaxpr/ppermute | solution.py:17
  1144.7 29.2 %copy-start.2 = (f32[1,16,128,256]{3,2,1,0:T(8,128)S(1)}, f32[1,16,128,256]{3,2,1,0:T(8,128)}, u32[]{:S(2)}) copy-start(f32[1,16,128,256]{3,2,1,0:T(8,128)} %get-tuple-element.624) | copy-start | bytes 6291460 | tf_op jit(solution)/shard_map/while
  1145.8 13.8 %collective-permute-start.2 = (f32[1,4,128,256]{3,2,1,0:T(8,128)}, f32[1,4,128,256]{3,2,1,0:T(8,128)S(1)}, u32[]{:S(2)}, u32[]{:S(2)}) collective-permute-start(f32[1,4,128,256]{3,2,1,0:T(8,128)} %get-tuple-element.570), channel_id=1, source_target_pairs={{0,1},{1,2},{2,3},{3,4},{4,5},{5,6},{6,7},{8,9},{9,10},{10,11},{11... | collective-permute-start | bytes 1572872 | tf_op jit(solution)/shard_map/while/body/eval_jaxpr/ppermute | solution.py:14
  1149.8 24.1 %collective-permute-start.3 = (f32[1,4,128,256]{3,2,1,0:T(8,128)}, f32[1,4,128,256]{3,2,1,0:T(8,128)S(1)}, u32[]{:S(2)}, u32[]{:S(2)}) collective-permute-start(f32[1,4,128,256]{3,2,1,0:T(8,128)} %get-tuple-element.571), channel_id=1, source_target_pairs={{1,0},{2,1},{3,2},{4,3},{5,4},{6,5},{7,6},{9,8},{10,9},{11,10},{12... | collective-permute-start | bytes 1572872 | tf_op jit(solution)/shard_map/while/body/eval_jaxpr/ppermute | solution.py:17
  1224.3 29.2 %copy-start.2 = (f32[1,16,128,256]{3,2,1,0:T(8,128)S(1)}, f32[1,16,128,256]{3,2,1,0:T(8,128)}, u32[]{:S(2)}) copy-start(f32[1,16,128,256]{3,2,1,0:T(8,128)} %get-tuple-element.624) | copy-start | bytes 6291460 | tf_op jit(solution)/shard_map/while
  1225.4 13.8 %collective-permute-start.2 = (f32[1,4,128,256]{3,2,1,0:T(8,128)}, f32[1,4,128,256]{3,2,1,0:T(8,128)S(1)}, u32[]{:S(2)}, u32[]{:S(2)}) collective-permute-start(f32[1,4,128,256]{3,2,1,0:T(8,128)} %get-tuple-element.570), channel_id=1, source_target_pairs={{0,1},{1,2},{2,3},{3,4},{4,5},{5,6},{6,7},{8,9},{9,10},{10,11},{11... | collective-permute-start | bytes 1572872 | tf_op jit(solution)/shard_map/while/body/eval_jaxpr/ppermute | solution.py:14
  1229.4 24.1 %collective-permute-start.3 = (f32[1,4,128,256]{3,2,1,0:T(8,128)}, f32[1,4,128,256]{3,2,1,0:T(8,128)S(1)}, u32[]{:S(2)}, u32[]{:S(2)}) collective-permute-start(f32[1,4,128,256]{3,2,1,0:T(8,128)} %get-tuple-element.571), channel_id=1, source_target_pairs={{1,0},{2,1},{3,2},{4,3},{5,4},{6,5},{7,6},{9,8},{10,9},{11,10},{12... | collective-permute-start | bytes 1572872 | tf_op jit(solution)/shard_map/while/body/eval_jaxpr/ppermute | solution.py:17
  (33 other events, 80.1 us)
Sparse Core Ops, SparseCore 0:
  1300.1 20.1 reduce-scatter.1
where the time goes:
time: 1330 us
  other arithmetic  526 us (40%)
  waiting for transfers between devices  451 us (34%)
  local copies, waits for them, and re-layouts  226 us (17%)
  starting transfers between devices  108 us (8%)
  between operations  13.4 us (1%)
    add x10, other arithmetic, backward(): adjoint = 2.0 * later - latest + laplace(extended)  292 us
    ppermute x20, waiting for transfers between devices, with_halo(): lax.ppermute(lax.slice_in_dim(block, 0, width, axis=dim), axis, backward)  248 us
    ppermute x20, waiting for transfers between devices, with_halo(): lax.ppermute(lax.slice_in_dim(block, block.shape[dim] - width, None, axis...  183 us
    scatter-add x20, other arithmetic, inject(): field.reshape(supers, -1).at[:, target].add(amounts, mode='drop')  85.2 us
    ppermute x20, starting transfers between devices, with_halo(): lax.ppermute(lax.slice_in_dim(block, block.shape[dim] - width, None, axis...  81.7 us
    while x160, local copies, waits for them, and re-layouts  80.6 us
    dynamic_update_slice x20, other arithmetic, shards(): lax.scan(forward, (fwd_prev, fwd_now), (wavelet, observed_all))  64 us
    gather x10, local copies, waits for them, and re-layouts, sample(): picked = field.reshape(supers, -1)[:, jnp.where(inside, local_index, 0)]  61.4 us
  transfers between devices with their start and end apart: 41, of which 39 were waited for; matrix products, arithmetic and copies ran while one was open for 1% of the time, Pallas kernels for 0%

commit v1 on v0

v1 whole, which is shorter than its diff:
```python
import functools

import jax
import jax.numpy as jnp
import numpy as np
from jax import lax
from jax.experimental import pallas as pl
from jax.experimental.pallas import tpu as pltpu
from jax.sharding import PartitionSpec as P

stencil_weights = (-205.0 / 72.0, 8.0 / 5.0, -1.0 / 5.0, 8.0 / 315.0, -1.0 / 560.0)
scaled_weights = (8064.0, -1008.0, 128.0, -9.0)
MESH = pl.DeviceIdType.MESH
f32 = jnp.float32
bf16 = jnp.bfloat16


def split(value):
    high = value.astype(bf16)
    low = (value - high.astype(f32)).astype(bf16)
    return high, low


def dot(a, b):
    return jnp.dot(a, b, preferred_element_type=f32)


def kernel(
    count,
    coef_in,
    prev_in,
    now_in,
    next_in,
    after_in,
    band,
    pick,
    place,
    shot_place,
    rec_depth,
    shot_amounts,
    observed,
    grad,
    field,
    adj,
    coef,
    history,
    sampled,
    misfit,
    in_local,
    in_send,
    in_recv,
    face_send,
    face_recv,
):
    steps = history.shape[0]
    layers, rows, depth = coef.shape
    half = layers // 2
    me = lax.axis_index("space")
    side = lax.rem(me, 2)
    partner = me + 1 - 2 * side
    has_left = me >= 2
    has_right = me < count - 2

    for slot in range(2):
        field[slot, 0:4] = jnp.zeros((4,) + field.shape[2:], f32)
        field[slot, layers + 4 : layers + 8] = jnp.zeros((4,) + field.shape[2:], f32)

        @pl.loop(0, layers)
        def _(x):
            field[slot, x + 4, 0:8] = jnp.zeros((8, depth), f32)
            field[slot, x + 4, rows + 8 : rows + 16] = jnp.zeros((8, depth), f32)

    barrier = pltpu.get_barrier_semaphore()
    pl.semaphore_signal(barrier, inc=1, device_id={"space": partner}, device_id_type=MESH)

    @pl.when(has_left)
    def _():
        pl.semaphore_signal(barrier, inc=1, device_id={"space": me - 2}, device_id_type=MESH)

    @pl.when(has_right)
    def _():
        pl.semaphore_signal(barrier, inc=1, device_id={"space": me + 2}, device_id_type=MESH)

    peers = 1 + jnp.where(has_left, 1, 0) + jnp.where(has_right, 1, 0)
    pl.semaphore_wait(barrier, peers)

    first = pl.multiple_of(side * half, half)
    keep = pl.multiple_of(side * rows, rows)
    give = pl.multiple_of(rows - side * rows, rows)
    targets = (
        (now_in, field.at[0, pl.ds(4 + first, half), pl.ds(8, rows)]),
        (prev_in, field.at[1, pl.ds(4 + first, half), pl.ds(8, rows)]),
        (coef_in, coef.at[pl.ds(first, half)]),
        (next_in, adj.at[0, pl.ds(first, half)]),
        (after_in, adj.at[1, pl.ds(first, half)]),
    )
    arriving = []
    for index, (source, target) in enumerate(targets):
        away = pltpu.make_async_remote_copy(
            src_ref=source.at[:, pl.ds(give, rows)],
            dst_ref=target,
            send_sem=in_send.at[index],
            recv_sem=in_recv.at[index],
            device_id={"space": partner},
            device_id_type=MESH,
        )
        here = pltpu.make_async_copy(
            source.at[:, pl.ds(keep, rows)], target, in_local.at[index]
        )
        away.start()
        here.start()
        arriving.append((away, here))

    def arrive(index):
        away, here = arriving[index]
        here.wait()
        away.wait()

    def faces(slot):
        near = pl.multiple_of((rows - 8) * (1 - side) + 8, 8)
        far = pl.multiple_of((rows + 8) * side, 8)
        inner = pl.ds(8, rows)
        to_left = pltpu.make_async_remote_copy(
            src_ref=field.at[slot, pl.ds(4, 4), inner],
            dst_ref=field.at[slot, pl.ds(layers + 4, 4), inner],
            send_sem=face_send.at[0, slot],
            recv_sem=face_recv.at[0, slot],
            device_id={"space": me - 2},
            device_id_type=MESH,
        )
        to_right = pltpu.make_async_remote_copy(
            src_ref=field.at[slot, pl.ds(layers, 4), inner],
            dst_ref=field.at[slot, pl.ds(0, 4), inner],
            send_sem=face_send.at[1, slot],
            recv_sem=face_recv.at[1, slot],
            device_id={"space": me + 2},
            device_id_type=MESH,
        )
        across = pltpu.make_async_remote_copy(
            src_ref=field.at[slot, pl.ds(4, layers), pl.ds(near, 8)],
            dst_ref=field.at[slot, pl.ds(4, layers), pl.ds(far, 8)],
            send_sem=face_send.at[2, slot],
            recv_sem=face_recv.at[2, slot],
            device_id={"space": partner},
            device_id_type=MESH,
        )
        return to_left, to_right, across

    def send_faces(slot):
        to_left, to_right, across = faces(slot)
        pl.when(has_left)(to_left.start)
        pl.when(has_right)(to_right.start)
        across.start()

    def receive_faces(slot):
        to_left, to_right, across = faces(slot)

        @pl.when(has_left)
        def _():
            to_left.wait_send()
            to_right.wait_recv()

        @pl.when(has_right)
        def _():
            to_right.wait_send()
            to_left.wait_recv()

        across.wait()

    block = 8
    lines = block * rows

    def flat(value):
        return value.reshape(lines, depth)

    def sample(slot, step):
        @pl.loop(0, layers // block)
        def _(c):
            part = field[slot, pl.ds(4 + c * block, block), 8 : rows + 8, :]
            high, low = split(flat(part))
            chooser = pick[c]
            found = dot(chooser, high) + dot(chooser, low)

            @pl.when(c == 0)
            def _():
                sampled[...] = found

            @pl.when(c > 0)
            def _():
                sampled[...] += found

        value = jnp.sum(sampled[...] * rec_depth[...], axis=1, keepdims=True)
        lane = lax.broadcasted_iota(jnp.int32, misfit.shape, 1)
        misfit[...] = jnp.where(lane == step, value, misfit[...])

    def depthwise(value):
        high, low = split(flat(value))
        along = dot(high, band[...]) + dot(low, band[...])
        return along.reshape(value.shape) * (1.0 / 5040.0) + (3.0 * stencil_weights[0]) * value

    def add_sides(slot, x, total):
        wide = field[slot, 4 + x]
        for offset in range(1, 5):
            beside = pltpu.roll(wide, offset, 0) + pltpu.roll(wide, rows + 16 - offset, 0)
            pair = field[slot, 4 + x + offset, 8 : rows + 8] + field[slot, 4 + x - offset, 8 : rows + 8]
            total = total + stencil_weights[offset] * (pair + beside[8 : rows + 8])
        return total

    arrive(0)
    arrive(1)
    arrive(2)
    misfit[...] = jnp.zeros_like(misfit)

    @pl.loop(0, steps)
    def _(step):
        slot = lax.rem(step, 2)
        other = 1 - slot
        send_faces(slot)

        @pl.when(step > 0)
        def _():
            sample(slot, step - 1)

        amount_high, amount_low = split(shot_amounts[step])

        @pl.loop(0, layers // block)
        def _(c):
            span = pl.ds(c * block, block)
            mid = pl.ds(4 + c * block, block)
            value = field[slot, mid, 8 : rows + 8, :]
            history[step, span] = depthwise(value)
            spots = shot_place[c]
            shots = dot(spots, amount_high) + dot(spots, amount_low)
            before = field[other, mid, 8 : rows + 8, :]
            field[other, mid, 8 : rows + 8, :] = 2.0 * value - before + shots.reshape(value.shape)

        receive_faces(slot)

        @pl.loop(0, layers)
        def _(x):
            total = add_sides(slot, x, history[step, x])
            history[step, x] = total
            field[other, 4 + x, 8 : rows + 8] += coef[x] * total

    last = steps % 2
    sample(last, steps - 1)
    misfit[...] = misfit[...] - observed[...]
    arrive(3)
    arrive(4)

    @pl.loop(0, layers)
    def _(x):
        field[last, 4 + x, 8 : rows + 8] = coef[x] * adj[0, x]
        grad[x] = jnp.zeros((rows, depth), f32)

    @pl.loop(0, steps)
    def _(back):
        slot = lax.rem(back + steps, 2)
        other = 1 - slot
        later = lax.rem(back, 2)
        latest = 1 - later
        step = steps - 1 - back
        send_faces(slot)
        lane = lax.broadcasted_iota(jnp.int32, misfit.shape, 1)
        amount = jnp.sum(jnp.where(lane == step, misfit[...], 0.0), axis=1, keepdims=True)
        amount_high, amount_low = split(amount * rec_depth[...])

        @pl.loop(0, layers // block)
        def _(c):
            span = pl.ds(c * block, block)
            value = field[slot, pl.ds(4 + c * block, block), 8 : rows + 8, :]
            spots = place[c]
            added = dot(spots, amount_high) + dot(spots, amount_low)
            adj[latest, span] = (
                2.0 * adj[later, span] - adj[latest, span] + depthwise(value) + added.reshape(value.shape)
            )

        receive_faces(slot)

        @pl.loop(0, layers)
        def _(x):
            total = add_sides(slot, x, adj[latest, x])
            adj[latest, x] = total
            field[other, 4 + x, 8 : rows + 8] = coef[x] * total
            grad[x] += total * history[step, x]


def shards(
    count, coef, fwd_prev, fwd_now, adj_next, adj_after, encode, wavelet, shot_cells, rec_cells, records
):
    thick, across, depth = coef.shape
    steps, shots = wavelet.shape
    receivers = rec_cells.shape[0]
    layers, rows = 2 * thick, across // 2
    me = lax.axis_index("space")
    block = 8
    chunks, lines = layers // block, block * rows

    def locate(cells):
        x = cells // (across * depth) - (me // 2) * layers
        y = (cells // depth) % across - (me % 2) * rows
        inside = (x >= 0) & (x < layers) & (y >= 0) & (y < rows)
        return jnp.where(inside, x * rows + y, -1), cells % depth

    rec_line, rec_z = locate(rec_cells)
    shot_line, shot_z = locate(shot_cells)
    width = -(-shots // 128) * 128
    shot_line = jnp.pad(shot_line, (0, width - shots), constant_values=-1)
    every = jnp.arange(layers * rows, dtype=jnp.int32).reshape(chunks, lines)
    pick = (rec_line[None, :, None] == every[:, None, :]).astype(bf16)
    place = (every[:, :, None] == rec_line[None, None, :]).astype(bf16)
    shot_place = (every[:, :, None] == shot_line[None, None, :]).astype(bf16)
    level = jnp.arange(depth, dtype=jnp.int32)
    rec_depth = (rec_z[:, None] == level[None, :]).astype(f32)
    amounts = encode[0][None, :] * wavelet
    shot_amounts = jnp.where(shot_z[None, :, None] == level[None, None, :], amounts[:, :, None], 0.0)
    shot_amounts = jnp.pad(shot_amounts, ((0, 0), (0, width - shots), (0, 0)))
    observed = jnp.pad(records[0].T, ((0, 0), (0, 128 - steps)))
    band = np.zeros((depth, depth), np.float32)
    for offset in range(1, 5):
        band += scaled_weights[offset - 1] * (np.eye(depth, k=offset) + np.eye(depth, k=-offset))

    vmem = pl.BlockSpec(memory_space=pltpu.VMEM)
    hbm = pl.BlockSpec(memory_space=pl.ANY)
    partial = pl.pallas_call(
        functools.partial(kernel, count),
        out_shape=jax.ShapeDtypeStruct((layers, rows, depth), f32),
        in_specs=[hbm] * 5 + [vmem] * 7,
        out_specs=vmem,
        scratch_shapes=[
            pltpu.VMEM((2, layers + 8, rows + 16, depth), f32),
            pltpu.VMEM((2, layers, rows, depth), f32),
            pltpu.VMEM((layers, rows, depth), f32),
            pltpu.VMEM((steps, layers, rows, depth), f32),
            pltpu.VMEM((receivers, depth), f32),
            pltpu.VMEM((receivers, 128), f32),
            pltpu.SemaphoreType.DMA((5,)),
            pltpu.SemaphoreType.DMA((5,)),
            pltpu.SemaphoreType.DMA((5,)),
            pltpu.SemaphoreType.DMA((3, 2)),
            pltpu.SemaphoreType.DMA((3, 2)),
        ],
        compiler_params=pltpu.CompilerParams(
            collective_id=0, has_side_effects=True, vmem_limit_bytes=60 * 1024 * 1024
        ),
    )(
        coef,
        fwd_prev[0],
        fwd_now[0],
        adj_next[0],
        adj_after[0],
        jnp.asarray(band, bf16),
        pick,
        place,
        shot_place,
        rec_depth,
        shot_amounts,
        observed,
    )
    summed = lax.psum_scatter(partial, "shot", scatter_dimension=0, tiled=True)
    moves = [
        (s * count + 2 * q + b, b * count + 2 * q + s)
        for q in range(count // 2)
        for b in range(2)
        for s in range(2)
    ]
    return lax.ppermute(summed, ("shot", "space"), moves)


def solution(mesh):
    placed = (
        P(("groups", "space"), None, None),
        P(("groups", "shot"), "space", None, None),
        P(("groups", "shot"), "space", None, None),
        P(("groups", "shot"), "space", None, None),
        P(("groups", "shot"), "space", None, None),
        P(("groups", "shot"), None),
        P("groups", None),
        P("groups"),
        P("groups"),
        P(("groups", "shot"), None, None),
    )
    return jax.shard_map(
        functools.partial(shards, mesh.shape["space"]),
        mesh=mesh,
        in_specs=placed,
        out_specs=P(("groups", "space"), "shot", None),
        check_vma=False,
    )
```

time: 1330 us -> 363 us (0.27)
  other arithmetic: 526 us -> 8.35 us
  waiting for transfers between devices: 451 us -> 32.4 us
  Pallas kernels: 0 us -> 302 us
  local copies, waits for them, and re-layouts: 226 us -> 3.26 us
  starting transfers between devices: 108 us -> 3.57 us
    ppermute x40 -> x1, waiting for transfers between devices: 431 us -> 12.7 us  [shards(): return lax.ppermute(summed, ('shot', 'space'), moves)]
    add x30 -> x0, other arithmetic: 344 us -> none  [the longest x10 292 us: backward(): adjoint = 2.0 * later - latest + laplace(extended)]
    pallas_call x0 -> x1, Pallas kernels: none -> 302 us  [shards(): pl.pallas_call(functools.partial(kernel, count), out_shape=jax.ShapeDtype...]
    ppermute x40 -> x1, starting transfers between devices: 108 us -> 3.57 us  [shards(): return lax.ppermute(summed, ('shot', 'space'), moves)]
    scatter-add x20 -> x0, other arithmetic: 85.2 us -> none  [inject(): field.reshape(supers, -1).at[:, target].add(amounts, mode='drop')]
    while x160 -> x0, local copies, waits for them, and re-layouts: 80.6 us -> none
    dynamic_update_slice x20 -> x0, other arithmetic: 64 us -> none  [shards(): lax.scan(forward, (fwd_prev, fwd_now), (wavelet, observed_all))]
    gather x10 -> x0, local copies, waits for them, and re-layouts: 61.4 us -> none  [sample(): picked = field.reshape(supers, -1)[:, jnp.where(inside, local_index, 0)]]
  transfers between devices with their start and end apart: 41 -> 2, of which waited for: 39 -> 2; matrix products, arithmetic and copies ran while one was open for 1% -> 0% of each run, Pallas kernels for 0% -> 0%
where the time goes in v1:
time: 363 us
  Pallas kernels  302 us (83%)
  waiting for transfers between devices  32.4 us (9%)
  between operations  13.5 us (4%)
  other arithmetic  8.35 us (2%)
    pallas_call x1, Pallas kernels, shards(): pl.pallas_call(functools.partial(kernel, count), out_shape=jax.ShapeDtype...  302 us
    reduce_scatter x1, waiting for transfers between devices, shards(): summed = lax.psum_scatter(partial, 'shot', scatter_dimension=0, tiled=True)  19.6 us
    ppermute x1, waiting for transfers between devices, shards(): return lax.ppermute(summed, ('shot', 'space'), moves)  12.7 us
  transfers between devices with their start and end apart: 2, of which 2 were waited for; matrix products, arithmetic and copies ran while one was open for 0% of the time, Pallas kernels for 0%

profile of v1, /device:TPU:1, one launch (start us, length us, event | category | flops | bytes accessed | tf_op | source)
XLA Modules:
  0.0 363.2 jit_solution(9160922833356788768)
XLA Ops:
  6.5 0.0 reduce-scatter.2.cloned.1.call-start
  6.5 0.7 add_select_fusion
  7.3 2.4 compare_convert_fusion.place
  9.7 0.0 copy-start.2
  9.7 0.0 copy-start
  9.7 0.0 copy-start.1
  9.7 0.0 copy-start.3
  9.7 2.7 compare_convert_fusion.1.pick
  12.4 0.0 copy-done.2
  12.4 0.1 iota_compare_fusion.1
  12.5 1.1 compare_convert_fusion.2.shot_place
  13.6 0.0 copy-done
  13.6 0.2 copy.12
  13.8 0.0 copy-done.1
  13.8 0.0 copy-done.3
  13.9 0.9 pad.14.observed
  14.7 0.1 broadcast_select_fusion
  14.9 1.2 pad.13.shot_amounts
  16.1 1.2 fusion.rec_depth
  17.2 302.2 %shard_map.109 = f32[32,64,256]{2,1,0:T(8,128)} custom-call(f32[16,128,256]{2,1,0:T(8,128)} %coef_in.1, f32[16,128,256]{2,1,0:T(8,128)} %bitcast.8, f32[16,128,256]{2,1,0:T(8,128)} %bitcast.9, f32[16,128,256]{2,1,0:T(8,128)} %bitcast.10, f32[16,128,256]{2,1,0:T(8,128)} %bitcast.11, bf16[256,256]{1,0:T(8,128)(2,1)} %constant.130.clone.band, ...), custom_call_target="tpu_custom_call" | custom-call | tf_op jit(solution)/shard_map/pallas_call | solution.py:325
  319.4 0.0 reduce-scatter.2.cloned.1.call-update
  319.4 19.6 %reduce-scatter.2.cloned.1.call-done = f32[16,64,256]{2,1,0:T(8,128)} async-done(((f32[32,64,256]{2,1,0:T(8,128)}), f32[16,64,256]{2,1,0:T(8,128)}) %reduce-scatter.2.cloned.1.call-update) | async-done | bytes 1048592 | tf_op jit(solution)/shard_map/reduce_scatter | solution.py:360
  339.1 3.6 collective-permute-start
  342.6 12.7 %collective-permute-done = f32[16,64,256]{2,1,0:T(8,128)S(1)} collective-permute-done((f32[16,64,256]{2,1,0:T(8,128)}, f32[16,64,256]{2,1,0:T(8,128)S(1)}, u32[]{:S(2)}, u32[]{:S(2)}) %collective-permute-start) | collective-permute-done | bytes 1048608 | tf_op jit(solution)/shard_map/ppermute | solution.py:367
  355.4 1.0 copy.14
  (4 shorter events, 0.0 us)
Async XLA Ops:
  6.5 332.5 %reduce-scatter.2.cloned.1.call-start = ((), (), s32[]{:S(2)}) async-start(), calls=%async_computation.1 | async-start | bytes 3145728 | tf_op jit(solution)/shard_map/reduce_scatter | solution.py:360
  9.7 2.7 copy-start.2
  9.7 3.9 %copy-start = (f32[1,10,1024]{2,0,1:T(1,128)S(1)}, f32[1,10,1024]{2,0,1:T(1,128)}, u32[]{:S(2)}) copy-start(f32[1,10,1024]{2,0,1:T(1,128)} %param.20) | copy-start | bytes 122884
  9.7 4.2 %copy-start.1 = (f32[10,64]{1,0:T(8,128)S(1)}, f32[10,64]{1,0:T(8,128)}, u32[]{:S(2)}) copy-start(f32[10,64]{1,0:T(8,128)} %param.17) | copy-start | bytes 7684
  9.7 4.2 %copy-start.3 = (f32[1,64]{1,0:T(1,128)S(1)}, f32[1,64]{1,0:T(1,128)}, u32[]{:S(2)}) copy-start(f32[1,64]{1,0:T(1,128)} %param.16) | copy-start | bytes 772
  339.1 16.3 %collective-permute-start = (f32[16,64,256]{2,1,0:T(8,128)}, f32[16,64,256]{2,1,0:T(8,128)S(1)}, u32[]{:S(2)}, u32[]{:S(2)}) collective-permute-start(f32[16,64,256]{2,1,0:T(8,128)} %reduce-scatter.2.cloned.1.call-done), channel_id=1, source_target_pairs={{0,0},{8,1},{1,8},{9,9},{2,2},{10,3},{3,10},{11,11},{4,4},{12,5},{... | collective-permute-start | bytes 3145736 | tf_op jit(solution)/shard_map/ppermute | solution.py:367
Sparse Core Ops, SparseCore 0:
  319.6 19.4 reduce-scatter.1

commit v2 on v1

--- a/solution.py
+++ b/solution.py
@@ -49,6 +49,8 @@
     in_local,
     in_send,
     in_recv,
+    twin_send,
+    twin_recv,
     face_send,
     face_recv,
 ):
@@ -56,6 +58,7 @@
     layers, rows, depth = coef.shape
     half = layers // 2
     me = lax.axis_index("space")
+    core = lax.axis_index("shot")
     side = lax.rem(me, 2)
     partner = me + 1 - 2 * side
     has_left = me >= 2
@@ -73,6 +76,8 @@
     barrier = pltpu.get_barrier_semaphore()
     pl.semaphore_signal(barrier, inc=1, device_id={"space": partner}, device_id_type=MESH)
 
+    pl.semaphore_signal(barrier, inc=1, device_id={"shot": 1 - core}, device_id_type=MESH)
+
     @pl.when(has_left)
     def _():
         pl.semaphore_signal(barrier, inc=1, device_id={"space": me - 2}, device_id_type=MESH)
@@ -81,12 +86,15 @@
     def _():
         pl.semaphore_signal(barrier, inc=1, device_id={"space": me + 2}, device_id_type=MESH)
 
-    peers = 1 + jnp.where(has_left, 1, 0) + jnp.where(has_right, 1, 0)
+    peers = 2 + jnp.where(has_left, 1, 0) + jnp.where(has_right, 1, 0)
     pl.semaphore_wait(barrier, peers)
 
     first = pl.multiple_of(side * half, half)
     keep = pl.multiple_of(side * rows, rows)
     give = pl.multiple_of(rows - side * rows, rows)
+    part = half // 2
+    mine = pl.multiple_of(core * part, part)
+    chunk = half // 8
     targets = (
         (now_in, field.at[0, pl.ds(4 + first, half), pl.ds(8, rows)]),
         (prev_in, field.at[1, pl.ds(4 + first, half), pl.ds(8, rows)]),
@@ -94,31 +102,47 @@
         (next_in, adj.at[0, pl.ds(first, half)]),
         (after_in, adj.at[1, pl.ds(first, half)]),
     )
-    arriving = []
-    for index, (source, target) in enumerate(targets):
-        away = pltpu.make_async_remote_copy(
-            src_ref=source.at[:, pl.ds(give, rows)],
-            dst_ref=target,
+
+    def swap(index, start, size):
+        source, target = targets[index]
+        return pltpu.make_async_remote_copy(
+            src_ref=source.at[pl.ds(start, size), pl.ds(give, rows)],
+            dst_ref=target.at[pl.ds(start, size)],
             send_sem=in_send.at[index],
             recv_sem=in_recv.at[index],
             device_id={"space": partner},
             device_id_type=MESH,
         )
-        here = pltpu.make_async_copy(
-            source.at[:, pl.ds(keep, rows)], target, in_local.at[index]
+
+    def stay(index):
+        source, target = targets[index]
+        return pltpu.make_async_copy(source.at[:, pl.ds(keep, rows)], target, in_local.at[index])
+
+    def arrive(index):
+        stay(index).wait()
+        swap(index, 0, half).wait()
+
+    swap(0, 0, half).start()
+    swap(1, 0, half).start()
+    swap(2, mine, part).start()
+    for index in range(5):
+        stay(index).start()
+
+    def share():
+        swap(2, mine, part).wait()
+        received = coef.at[pl.ds(half - first + mine, part)]
+        return pltpu.make_async_remote_copy(
+            src_ref=received,
+            dst_ref=received,
+            send_sem=twin_send,
+            recv_sem=twin_recv,
+            device_id={"shot": 1 - core},
+            device_id_type=MESH,
         )
-        away.start()
-        here.start()
-        arriving.append((away, here))
-
-    def arrive(index):
-        away, here = arriving[index]
-        here.wait()
-        away.wait()
 
     def faces(slot):
-        near = pl.multiple_of((rows - 8) * (1 - side) + 8, 8)
-        far = pl.multiple_of((rows + 8) * side, 8)
+        near = (rows - 4) * (1 - side) + 8
+        far = rows * side + 8 * side + 4 * (1 - side)
         inner = pl.ds(8, rows)
         to_left = pltpu.make_async_remote_copy(
             src_ref=field.at[slot, pl.ds(4, 4), inner],
@@ -137,8 +161,8 @@
             device_id_type=MESH,
         )
         across = pltpu.make_async_remote_copy(
-            src_ref=field.at[slot, pl.ds(4, layers), pl.ds(near, 8)],
-            dst_ref=field.at[slot, pl.ds(4, layers), pl.ds(far, 8)],
+            src_ref=field.at[slot, pl.ds(4, layers), pl.ds(near, 4)],
+            dst_ref=field.at[slot, pl.ds(4, layers), pl.ds(far, 4)],
             send_sem=face_send.at[2, slot],
             recv_sem=face_recv.at[2, slot],
             device_id={"space": partner},
@@ -173,77 +197,116 @@
     def flat(value):
         return value.reshape(lines, depth)
 
-    def sample(slot, step):
-        @pl.loop(0, layers // block)
-        def _(c):
-            part = field[slot, pl.ds(4 + c * block, block), 8 : rows + 8, :]
-            high, low = split(flat(part))
-            chooser = pick[c]
-            found = dot(chooser, high) + dot(chooser, low)
-
-            @pl.when(c == 0)
-            def _():
-                sampled[...] = found
-
-            @pl.when(c > 0)
-            def _():
-                sampled[...] += found
-
+    def store_sample(step):
         value = jnp.sum(sampled[...] * rec_depth[...], axis=1, keepdims=True)
         lane = lax.broadcasted_iota(jnp.int32, misfit.shape, 1)
         misfit[...] = jnp.where(lane == step, value, misfit[...])
 
-    def depthwise(value):
-        high, low = split(flat(value))
+    def add_sample(c, high, low):
+        chooser = pick[c]
+        found = dot(chooser, high) + dot(chooser, low)
+
+        @pl.when(c == 0)
+        def _():
+            sampled[...] = found
+
+        @pl.when(c > 0)
+        def _():
+            sampled[...] += found
+
+    def depthwise(value, high, low):
         along = dot(high, band[...]) + dot(low, band[...])
         return along.reshape(value.shape) * (1.0 / 5040.0) + (3.0 * stencil_weights[0]) * value
 
-    def add_sides(slot, x, total):
-        wide = field[slot, 4 + x]
+    def add_sides(slot, x, low, tall, total):
+        wide = field[slot, 4 + x, pl.ds(low, tall + 16)]
+        here = pl.ds(pl.multiple_of(low + 8, 8), tall)
         for offset in range(1, 5):
-            beside = pltpu.roll(wide, offset, 0) + pltpu.roll(wide, rows + 16 - offset, 0)
-            pair = field[slot, 4 + x + offset, 8 : rows + 8] + field[slot, 4 + x - offset, 8 : rows + 8]
-            total = total + stencil_weights[offset] * (pair + beside[8 : rows + 8])
+            beside = pltpu.roll(wide, offset, 0) + pltpu.roll(wide, tall + 16 - offset, 0)
+            pair = field[slot, 4 + x + offset, here] + field[slot, 4 + x - offset, here]
+            total = total + stencil_weights[offset] * (pair + beside[8 : tall + 8])
         return total
 
+    inner_low = pl.multiple_of(8 * side, 8)
+    edge_low = pl.multiple_of((rows - 8) * (1 - side), 8)
+
+    def rim(unit):
+        @pl.loop(0, 4)
+        def _(x):
+            unit(x, 0, rows)
+            unit(layers - 4 + x, 0, rows)
+
+        @pl.loop(1, layers // 4 - 1)
+        def _(x):
+            for inside in range(4):
+                unit(4 * x + inside, edge_low, 8)
+
+    def interior(unit):
+        @pl.loop(4, layers - 4)
+        def _(x):
+            unit(x, inner_low, rows - 8)
+
+    misfit[...] = jnp.zeros_like(misfit)
     arrive(0)
+    send_faces(0)
     arrive(1)
-    arrive(2)
-    misfit[...] = jnp.zeros_like(misfit)
 
     @pl.loop(0, steps)
     def _(step):
         slot = lax.rem(step, 2)
         other = 1 - slot
-        send_faces(slot)
-
-        @pl.when(step > 0)
-        def _():
-            sample(slot, step - 1)
-
         amount_high, amount_low = split(shot_amounts[step])
+
+        @pl.when(step < 8)
+        def _():
+            swap(3, step * chunk, chunk).start()
+            swap(4, step * chunk, chunk).start()
 
         @pl.loop(0, layers // block)
         def _(c):
             span = pl.ds(c * block, block)
             mid = pl.ds(4 + c * block, block)
             value = field[slot, mid, 8 : rows + 8, :]
-            history[step, span] = depthwise(value)
+            high, low = split(flat(value))
+            history[step, span] = depthwise(value, high, low)
             spots = shot_place[c]
             shots = dot(spots, amount_high) + dot(spots, amount_low)
             before = field[other, mid, 8 : rows + 8, :]
             field[other, mid, 8 : rows + 8, :] = 2.0 * value - before + shots.reshape(value.shape)
+            add_sample(c, high, low)
+
+        store_sample(step - 1)
+
+        @pl.when(step == 0)
+        def _():
+            stay(2).wait()
+            passed = share()
+            passed.start()
+            passed.wait()
 
         receive_faces(slot)
 
-        @pl.loop(0, layers)
-        def _(x):
-            total = add_sides(slot, x, history[step, x])
-            history[step, x] = total
-            field[other, 4 + x, 8 : rows + 8] += coef[x] * total
+        def unit(x, low, tall):
+            mine = pl.ds(low, tall)
+            total = add_sides(slot, x, low, tall, history[step, x, mine])
+            history[step, x, mine] = total
+            field[other, 4 + x, pl.ds(pl.multiple_of(low + 8, 8), tall)] += coef[x, mine] * total
+
+        rim(unit)
+
+        @pl.when(step < steps - 1)
+        def _():
+            send_faces(other)
+
+        interior(unit)
 
     last = steps % 2
-    sample(last, steps - 1)
+
+    @pl.loop(0, layers // block)
+    def _(c):
+        add_sample(c, *split(flat(field[last, pl.ds(4 + c * block, block), 8 : rows + 8, :])))
+
+    store_sample(steps - 1)
     misfit[...] = misfit[...] - observed[...]
     arrive(3)
     arrive(4)
@@ -252,6 +315,8 @@
     def _(x):
         field[last, 4 + x, 8 : rows + 8] = coef[x] * adj[0, x]
         grad[x] = jnp.zeros((rows, depth), f32)
+
+    send_faces(last)
 
     @pl.loop(0, steps)
     def _(back):
@@ -260,7 +325,6 @@
         later = lax.rem(back, 2)
         latest = 1 - later
         step = steps - 1 - back
-        send_faces(slot)
         lane = lax.broadcasted_iota(jnp.int32, misfit.shape, 1)
         amount = jnp.sum(jnp.where(lane == step, misfit[...], 0.0), axis=1, keepdims=True)
         amount_high, amount_low = split(amount * rec_depth[...])
@@ -272,17 +336,28 @@
             spots = place[c]
             added = dot(spots, amount_high) + dot(spots, amount_low)
             adj[latest, span] = (
-                2.0 * adj[later, span] - adj[latest, span] + depthwise(value) + added.reshape(value.shape)
+                2.0 * adj[later, span]
+                - adj[latest, span]
+                + depthwise(value, *split(flat(value)))
+                + added.reshape(value.shape)
             )
 
         receive_faces(slot)
 
-        @pl.loop(0, layers)
-        def _(x):
-            total = add_sides(slot, x, adj[latest, x])
-            adj[latest, x] = total
-            field[other, 4 + x, 8 : rows + 8] = coef[x] * total
-            grad[x] += total * history[step, x]
+        def unit(x, low, tall):
+            mine = pl.ds(low, tall)
+            total = add_sides(slot, x, low, tall, adj[latest, x, mine])
+            adj[latest, x, mine] = total
+            field[other, 4 + x, pl.ds(pl.multiple_of(low + 8, 8), tall)] = coef[x, mine] * total
+            grad[x, mine] += total * history[step, x, mine]
+
+        rim(unit)
+
+        @pl.when(back < steps - 1)
+        def _():
+            send_faces(other)
+
+        interior(unit)
 
 
 def shards(
@@ -337,6 +412,8 @@
             pltpu.SemaphoreType.DMA((5,)),
             pltpu.SemaphoreType.DMA((5,)),
             pltpu.SemaphoreType.DMA((5,)),
+            pltpu.SemaphoreType.DMA,
+            pltpu.SemaphoreType.DMA,
             pltpu.SemaphoreType.DMA((3, 2)),
             pltpu.SemaphoreType.DMA((3, 2)),
         ],

time: 363 us -> 277 us (0.76)
  Pallas kernels: 302 us -> 225 us
  waiting for transfers between devices: 32.4 us -> 23.9 us
    pallas_call x1, Pallas kernels: 302 us -> 225 us  [shards(): pl.pallas_call(functools.partial(kernel, count), out_shape=jax.ShapeDtype...]
    reduce_scatter x1, waiting for transfers between devices: 19.6 us -> 11.2 us  [shards(): summed = lax.psum_scatter(partial, 'shot', scatter_dimension=0, tiled=True)]
where the time goes in v2:
time: 277 us
  Pallas kernels  225 us (81%)
  waiting for transfers between devices  23.9 us (9%)
  between operations  13.5 us (5%)
  other arithmetic  8.35 us (3%)
  starting transfers between devices  3.55 us (1%)
  local copies, waits for them, and re-layouts  3.26 us (1%)
    pallas_call x1, Pallas kernels, shards(): pl.pallas_call(functools.partial(kernel, count), out_shape=jax.ShapeDtype...  225 us
    ppermute x1, waiting for transfers between devices, shards(): return lax.ppermute(summed, ('shot', 'space'), moves)  12.8 us
    reduce_scatter x1, waiting for transfers between devices, shards(): summed = lax.psum_scatter(partial, 'shot', scatter_dimension=0, tiled=True)  11.2 us
  transfers between devices with their start and end apart: 2, of which 2 were waited for; matrix products, arithmetic and copies ran while one was open for 0% of the time, Pallas kernels for 0%

profile of v2, /device:TPU:1, one launch (start us, length us, event | category | flops | bytes accessed | tf_op | source)
XLA Modules:
  0.0 277.1 jit_solution(6367545638361811653)
XLA Ops:
  6.5 0.0 reduce-scatter.2.cloned.1.call-start
  6.5 0.7 add_select_fusion
  7.3 2.4 compare_convert_fusion.place
  9.7 0.0 copy-start.2
  9.7 0.0 copy-start
  9.7 0.0 copy-start.1
  9.7 0.0 copy-start.3
  9.7 2.7 compare_convert_fusion.1.pick
  12.4 0.0 copy-done.2
  12.4 0.1 iota_compare_fusion.1
  12.5 1.1 compare_convert_fusion.2.shot_place
  13.6 0.0 copy-done
  13.6 0.2 copy.12
  13.8 0.0 copy-done.1
  13.8 0.0 copy-done.3
  13.9 0.9 pad.14.observed
  14.7 0.1 broadcast_select_fusion
  14.9 1.2 pad.13.shot_amounts
  16.1 1.2 fusion.rec_depth
  17.2 224.6 %shard_map.109 = f32[32,64,256]{2,1,0:T(8,128)} custom-call(f32[16,128,256]{2,1,0:T(8,128)} %coef_in.1, f32[16,128,256]{2,1,0:T(8,128)} %bitcast.8, f32[16,128,256]{2,1,0:T(8,128)} %bitcast.9, f32[16,128,256]{2,1,0:T(8,128)} %bitcast.10, f32[16,128,256]{2,1,0:T(8,128)} %bitcast.11, bf16[256,256]{1,0:T(8,128)(2,1)} %constant.130.clone.band, ...), custom_call_target="tpu_custom_call" | custom-call | tf_op jit(solution)/shard_map/pallas_call | solution.py:400
  241.8 0.0 reduce-scatter.2.cloned.1.call-update
  241.8 11.2 %reduce-scatter.2.cloned.1.call-done = f32[16,64,256]{2,1,0:T(8,128)} async-done(((f32[32,64,256]{2,1,0:T(8,128)}), f32[16,64,256]{2,1,0:T(8,128)}) %reduce-scatter.2.cloned.1.call-update) | async-done | bytes 1048592 | tf_op jit(solution)/shard_map/reduce_scatter | solution.py:437
  253.0 3.6 %collective-permute-start = (f32[16,64,256]{2,1,0:T(8,128)}, f32[16,64,256]{2,1,0:T(8,128)S(1)}, u32[]{:S(2)}, u32[]{:S(2)}) collective-permute-start(f32[16,64,256]{2,1,0:T(8,128)} %reduce-scatter.2.cloned.1.call-done), channel_id=1, source_target_pairs={{0,0},{8,1},{1,8},{9,9},{2,2},{10,3},{3,10},{11,11},{4,4},{12,5},{... | collective-permute-start | bytes 3145736 | tf_op jit(solution)/shard_map/ppermute | solution.py:444
  256.6 12.8 %collective-permute-done = f32[16,64,256]{2,1,0:T(8,128)S(1)} collective-permute-done((f32[16,64,256]{2,1,0:T(8,128)}, f32[16,64,256]{2,1,0:T(8,128)S(1)}, u32[]{:S(2)}, u32[]{:S(2)}) %collective-permute-start) | collective-permute-done | bytes 1048608 | tf_op jit(solution)/shard_map/ppermute | solution.py:444
  269.3 1.0 copy.14
  (4 shorter events, 0.0 us)
Async XLA Ops:
  6.5 246.5 %reduce-scatter.2.cloned.1.call-start = ((), (), s32[]{:S(2)}) async-start(), calls=%async_computation.1 | async-start | bytes 3145728 | tf_op jit(solution)/shard_map/reduce_scatter | solution.py:437
  9.7 2.7 copy-start.2
  9.7 3.9 %copy-start = (f32[1,10,1024]{2,0,1:T(1,128)S(1)}, f32[1,10,1024]{2,0,1:T(1,128)}, u32[]{:S(2)}) copy-start(f32[1,10,1024]{2,0,1:T(1,128)} %param.20) | copy-start | bytes 122884
  9.7 4.2 %copy-start.1 = (f32[10,64]{1,0:T(8,128)S(1)}, f32[10,64]{1,0:T(8,128)}, u32[]{:S(2)}) copy-start(f32[10,64]{1,0:T(8,128)} %param.17) | copy-start | bytes 7684
  9.7 4.2 %copy-start.3 = (f32[1,64]{1,0:T(1,128)S(1)}, f32[1,64]{1,0:T(1,128)}, u32[]{:S(2)}) copy-start(f32[1,64]{1,0:T(1,128)} %param.16) | copy-start | bytes 772
  253.0 16.3 %collective-permute-start = (f32[16,64,256]{2,1,0:T(8,128)}, f32[16,64,256]{2,1,0:T(8,128)S(1)}, u32[]{:S(2)}, u32[]{:S(2)}) collective-permute-start(f32[16,64,256]{2,1,0:T(8,128)} %reduce-scatter.2.cloned.1.call-done), channel_id=1, source_target_pairs={{0,0},{8,1},{1,8},{9,9},{2,2},{10,3},{3,10},{11,11},{4,4},{12,5},{... | collective-permute-start | bytes 3145736 | tf_op jit(solution)/shard_map/ppermute | solution.py:444
Sparse Core Ops, SparseCore 0:
  242.0 11.0 reduce-scatter.1

commit v3 on v2

--- a/solution.py
+++ b/solution.py
@@ -33,13 +33,20 @@
     next_in,
     after_in,
     band,
+    rec_line,
+    rec_column,
+    rec_level,
+    shot_line,
+    shot_level,
+    shot_amounts,
+    observed,
+    out,
     pick,
     place,
     shot_place,
     rec_depth,
-    shot_amounts,
-    observed,
     grad,
+    twin_grad,
     field,
     adj,
     coef,
@@ -53,6 +60,10 @@
     twin_recv,
     face_send,
     face_recv,
+    half_send,
+    half_recv,
+    out_send,
+    out_recv,
 ):
     steps = history.shape[0]
     layers, rows, depth = coef.shape
@@ -86,7 +97,14 @@
     def _():
         pl.semaphore_signal(barrier, inc=1, device_id={"space": me + 2}, device_id_type=MESH)
 
-    peers = 2 + jnp.where(has_left, 1, 0) + jnp.where(has_right, 1, 0)
+    crossed = side != core
+    owner = {"space": partner, "shot": 1 - core}
+
+    @pl.when(crossed)
+    def _():
+        pl.semaphore_signal(barrier, inc=1, device_id=owner, device_id_type=MESH)
+
+    peers = 2 + jnp.where(crossed, 1, 0) + jnp.where(has_left, 1, 0) + jnp.where(has_right, 1, 0)
     pl.semaphore_wait(barrier, peers)
 
     first = pl.multiple_of(side * half, half)
@@ -247,6 +265,21 @@
             unit(x, inner_low, rows - 8)
 
     misfit[...] = jnp.zeros_like(misfit)
+
+    def one_hot(index, shape, axis, start, kind):
+        hit = lax.broadcasted_iota(jnp.int32, shape, axis) + start == index
+        return jnp.where(hit, 1.0, 0.0).astype(kind)
+
+    receivers, shots_held = rec_depth.shape[0], shot_place.shape[2]
+    rec_depth[...] = one_hot(rec_level[...], rec_depth.shape, 1, 0, f32)
+
+    @pl.loop(0, layers // block)
+    def _(c):
+        start = c * lines
+        pick[c] = one_hot(rec_column[...], (receivers, lines), 1, start, bf16)
+        place[c] = one_hot(rec_line[...], (lines, receivers), 0, start, bf16)
+        shot_place[c] = one_hot(shot_line[...], (lines, shots_held), 0, start, bf16)
+
     arrive(0)
     send_faces(0)
     arrive(1)
@@ -255,7 +288,10 @@
     def _(step):
         slot = lax.rem(step, 2)
         other = 1 - slot
-        amount_high, amount_low = split(shot_amounts[step])
+        shot_lane = lax.broadcasted_iota(jnp.int32, shot_amounts.shape, 1)
+        shot_amount = jnp.sum(jnp.where(shot_lane == step, shot_amounts[...], 0.0), axis=1, keepdims=True)
+        shot_depth = one_hot(shot_level[...], (shots_held, depth), 1, 0, f32)
+        amount_high, amount_low = split(shot_amount * shot_depth)
 
         @pl.when(step < 8)
         def _():
@@ -351,13 +387,69 @@
             field[other, 4 + x, pl.ds(pl.multiple_of(low + 8, 8), tall)] = coef[x, mine] * total
             grad[x, mine] += total * history[step, x, mine]
 
-        rim(unit)
-
         @pl.when(back < steps - 1)
         def _():
+            rim(unit)
             send_faces(other)
-
-        interior(unit)
+            interior(unit)
+
+        @pl.when(back == steps - 1)
+        def _():
+            own = pl.multiple_of(core * half, half)
+            handed = half - own
+
+            @pl.loop(0, half)
+            def _(x):
+                unit(handed + x, 0, rows)
+
+            halves = pltpu.make_async_remote_copy(
+                src_ref=grad.at[pl.ds(handed, half)],
+                dst_ref=twin_grad,
+                send_sem=half_send,
+                recv_sem=half_recv,
+                device_id={"shot": 1 - core},
+                device_id_type=MESH,
+            )
+            halves.start()
+
+            @pl.loop(0, half)
+            def _(x):
+                unit(own + x, 0, rows)
+
+            halves.wait()
+
+            @pl.when(jnp.logical_not(crossed))
+            def _():
+                @pl.loop(0, half)
+                def _(x):
+                    out[x] = grad[own + x] + twin_grad[x]
+
+            @pl.when(crossed)
+            def _():
+                size = half // 4
+
+                @pl.loop(0, 4)
+                def _(c):
+                    span = pl.ds(c * size, size)
+                    twin_grad[span] = grad[pl.ds(own + c * size, size)] + twin_grad[span]
+                    piece = pltpu.make_async_remote_copy(
+                        src_ref=twin_grad.at[span],
+                        dst_ref=out.at[span],
+                        send_sem=out_send,
+                        recv_sem=out_recv,
+                        device_id=owner,
+                        device_id_type=MESH,
+                    )
+                    piece.start()
+
+                pltpu.make_async_remote_copy(
+                    src_ref=twin_grad,
+                    dst_ref=out,
+                    send_sem=out_send,
+                    recv_sem=out_recv,
+                    device_id=owner,
+                    device_id_type=MESH,
+                ).wait()
 
 
 def shards(
@@ -381,15 +473,8 @@
     shot_line, shot_z = locate(shot_cells)
     width = -(-shots // 128) * 128
     shot_line = jnp.pad(shot_line, (0, width - shots), constant_values=-1)
-    every = jnp.arange(layers * rows, dtype=jnp.int32).reshape(chunks, lines)
-    pick = (rec_line[None, :, None] == every[:, None, :]).astype(bf16)
-    place = (every[:, :, None] == rec_line[None, None, :]).astype(bf16)
-    shot_place = (every[:, :, None] == shot_line[None, None, :]).astype(bf16)
-    level = jnp.arange(depth, dtype=jnp.int32)
-    rec_depth = (rec_z[:, None] == level[None, :]).astype(f32)
-    amounts = encode[0][None, :] * wavelet
-    shot_amounts = jnp.where(shot_z[None, :, None] == level[None, None, :], amounts[:, :, None], 0.0)
-    shot_amounts = jnp.pad(shot_amounts, ((0, 0), (0, width - shots), (0, 0)))
+    amounts = jnp.pad((encode * wavelet).T, ((0, width - shots), (0, 128 - steps)))
+    shot_z = jnp.pad(shot_z, (0, width - shots))
     observed = jnp.pad(records[0].T, ((0, 0), (0, 128 - steps)))
     band = np.zeros((depth, depth), np.float32)
     for offset in range(1, 5):
@@ -397,12 +482,18 @@
 
     vmem = pl.BlockSpec(memory_space=pltpu.VMEM)
     hbm = pl.BlockSpec(memory_space=pl.ANY)
-    partial = pl.pallas_call(
+    return pl.pallas_call(
         functools.partial(kernel, count),
-        out_shape=jax.ShapeDtypeStruct((layers, rows, depth), f32),
-        in_specs=[hbm] * 5 + [vmem] * 7,
+        out_shape=jax.ShapeDtypeStruct((thick, rows, depth), f32),
+        in_specs=[hbm] * 5 + [vmem] * 8,
         out_specs=vmem,
         scratch_shapes=[
+            pltpu.VMEM((chunks, receivers, lines), bf16),
+            pltpu.VMEM((chunks, lines, receivers), bf16),
+            pltpu.VMEM((chunks, lines, width), bf16),
+            pltpu.VMEM((receivers, depth), f32),
+            pltpu.VMEM((layers, rows, depth), f32),
+            pltpu.VMEM((thick, rows, depth), f32),
             pltpu.VMEM((2, layers + 8, rows + 16, depth), f32),
             pltpu.VMEM((2, layers, rows, depth), f32),
             pltpu.VMEM((layers, rows, depth), f32),
@@ -416,6 +507,10 @@
             pltpu.SemaphoreType.DMA,
             pltpu.SemaphoreType.DMA((3, 2)),
             pltpu.SemaphoreType.DMA((3, 2)),
+            pltpu.SemaphoreType.DMA,
+            pltpu.SemaphoreType.DMA,
+            pltpu.SemaphoreType.DMA,
+            pltpu.SemaphoreType.DMA,
         ],
         compiler_params=pltpu.CompilerParams(
             collective_id=0, has_side_effects=True, vmem_limit_bytes=60 * 1024 * 1024
@@ -427,21 +522,14 @@
         adj_next[0],
         adj_after[0],
         jnp.asarray(band, bf16),
-        pick,
-        place,
-        shot_place,
-        rec_depth,
-        shot_amounts,
+        rec_line[None, :],
+        rec_line[:, None],
+        rec_z[:, None],
+        shot_line[None, :],
+        shot_z[:, None],
+        amounts,
         observed,
     )
-    summed = lax.psum_scatter(partial, "shot", scatter_dimension=0, tiled=True)
-    moves = [
-        (s * count + 2 * q + b, b * count + 2 * q + s)
-        for q in range(count // 2)
-        for b in range(2)
-        for s in range(2)
-    ]
-    return lax.ppermute(summed, ("shot", "space"), moves)
 
 
 def solution(mesh):

time: 277 us -> 251 us (0.906)
  waiting for transfers between devices: 23.9 us -> 0 us
  Pallas kernels: 225 us -> 240 us
  between operations: 13.5 us -> 0.03 us
  other arithmetic: 8.35 us -> 2.11 us
  local copies, waits for them, and re-layouts: 3.26 us -> 8.8 us
  starting transfers between devices: 3.55 us -> 0 us
    pallas_call x1, Pallas kernels: 225 us -> 240 us  [shards(): pl.pallas_call(functools.partial(kernel, count), out_shape=jax.ShapeDtype...]
    ppermute x1 -> x0, waiting for transfers between devices: 12.8 us -> none  [shards(): return lax.ppermute(summed, ('shot', 'space'), moves)]
    reduce_scatter x1 -> x0, waiting for transfers between devices: 11.2 us -> none  [shards(): summed = lax.psum_scatter(partial, 'shot', scatter_dimension=0, tiled=True)]
    convert_element_type x4 -> x0, other arithmetic: 7.39 us -> none  [the longest x1 2.68 us: shards(): pick = (rec_line[None, :, None] == every[:, None, :]).astype(bf16)]
    ppermute x1 -> x0, starting transfers between devices: 3.55 us -> none  [shards(): return lax.ppermute(summed, ('shot', 'space'), moves)]
    broadcast_in_dim x0 -> x4, local copies, waits for them, and re-layouts: none -> 3.27 us  [the longest x2 1.21 us: shards(): shot_z[:, None]]
    unnamed x10 -> x5, local copies, waits for them, and re-layouts: 1.2 us -> 4.07 us
  transfers between devices with their start and end apart: 2 -> 0, of which waited for: 2 -> 0; matrix products, arithmetic and copies ran while one was open for 0% -> 0% of each run, Pallas kernels for 0% -> 0%
where the time goes in v3:
time: 251 us
  Pallas kernels  240 us (96%)
  local copies, waits for them, and re-layouts  8.8 us (4%)
    pallas_call x1, Pallas kernels, shards(): pl.pallas_call(functools.partial(kernel, count), out_shape=jax.ShapeDtype...  240 us

profile of v3, /device:TPU:1, one launch (start us, length us, event | category | flops | bytes accessed | tf_op | source)
XLA Modules:
  0.0 250.8 jit_solution(16753419705817824003)
XLA Ops:
  0.0 0.7 and_select_fusion
  0.7 0.5 pad_bitcast_fusion
  1.2 0.7 add_select_fusion
  1.9 0.0 copy-start
  1.9 0.8 copy.21
  2.7 0.7 multiply_bitcast_fusion
  3.4 0.6 pad.17.shot_amounts
  4.0 0.7 copy.25.shot_level
  4.7 1.0 copy.24.rec_level
  5.8 1.0 copy.23.rec_column
  6.8 1.0 copy.22
  7.8 0.8 pad.18.observed
  8.6 0.0 copy-done
  8.6 239.9 %shard_map.109 = f32[16,64,256]{2,1,0:T(8,128)} custom-call(f32[16,128,256]{2,1,0:T(8,128)} %coef_in.1, f32[16,128,256]{2,1,0:T(8,128)} %bitcast.17, f32[16,128,256]{2,1,0:T(8,128)} %bitcast.18, f32[16,128,256]{2,1,0:T(8,128)} %bitcast.19, f32[16,128,256]{2,1,0:T(8,128)} %bitcast.20, bf16[256,256]{1,0:T(8,128)(2,1)} %constant.124.clone.band, ...), custom_call_target="tpu_custom_call" | custom-call | tf_op jit(solution)/shard_map/pallas_call | solution.py:485
  248.5 2.3 copy.27
Async XLA Ops:
  1.9 6.8 %copy-start = (s32[1024]{0:T(1024)}, s32[1024]{0:T(1024)S(1)}, u32[]{:S(2)}) copy-start(s32[1024]{0:T(1024)S(1)} %get-tuple-element.6) | copy-start | bytes 12292

commit v4 on v3

--- a/solution.py
+++ b/solution.py
@@ -33,6 +33,7 @@
     next_in,
     after_in,
     band,
+    row_band,
     rec_line,
     rec_column,
     rec_level,
@@ -239,10 +240,12 @@
     def add_sides(slot, x, low, tall, total):
         wide = field[slot, 4 + x, pl.ds(low, tall + 16)]
         here = pl.ds(pl.multiple_of(low + 8, 8), tall)
+        high, rest = split(wide)
+        mixer = row_band[0:tall, 0 : tall + 16].astype(bf16)
+        total = total + (dot(mixer, high) + dot(mixer, rest)) * (1.0 / 5040.0)
         for offset in range(1, 5):
-            beside = pltpu.roll(wide, offset, 0) + pltpu.roll(wide, tall + 16 - offset, 0)
             pair = field[slot, 4 + x + offset, here] + field[slot, 4 + x - offset, here]
-            total = total + stencil_weights[offset] * (pair + beside[8 : tall + 8])
+            total = total + stencil_weights[offset] * pair
         return total
 
     inner_low = pl.multiple_of(8 * side, 8)
@@ -260,9 +263,10 @@
                 unit(4 * x + inside, edge_low, 8)
 
     def interior(unit):
-        @pl.loop(4, layers - 4)
+        @pl.loop(2, layers // 2 - 2)
         def _(x):
-            unit(x, inner_low, rows - 8)
+            unit(2 * x, inner_low, rows - 8)
+            unit(2 * x + 1, inner_low, rows - 8)
 
     misfit[...] = jnp.zeros_like(misfit)
 
@@ -480,12 +484,17 @@
     for offset in range(1, 5):
         band += scaled_weights[offset - 1] * (np.eye(depth, k=offset) + np.eye(depth, k=-offset))
 
+    row_band = np.zeros((rows, rows + 16), np.float32)
+    for offset in range(1, 5):
+        for shift in (offset, -offset):
+            row_band += scaled_weights[offset - 1] * np.eye(rows, rows + 16, k=8 + shift)
+
     vmem = pl.BlockSpec(memory_space=pltpu.VMEM)
     hbm = pl.BlockSpec(memory_space=pl.ANY)
     return pl.pallas_call(
         functools.partial(kernel, count),
         out_shape=jax.ShapeDtypeStruct((thick, rows, depth), f32),
-        in_specs=[hbm] * 5 + [vmem] * 8,
+        in_specs=[hbm] * 5 + [vmem] * 9,
         out_specs=vmem,
         scratch_shapes=[
             pltpu.VMEM((chunks, receivers, lines), bf16),
@@ -522,6 +531,7 @@
         adj_next[0],
         adj_after[0],
         jnp.asarray(band, bf16),
+        jnp.asarray(row_band, f32),
         rec_line[None, :],
         rec_line[:, None],
         rec_z[:, None],

time: 251 us -> 356 us (1.42)
  Pallas kernels: 240 us -> 345 us
    pallas_call x1, Pallas kernels: 240 us -> 345 us  [shards(): pl.pallas_call(functools.partial(kernel, count), out_shape=jax.ShapeDtype...]
where the time goes in v4:
time: 356 us; the launch traced here: 355 us
  Pallas kernels  345 us (97%)
  local copies, waits for them, and re-layouts  8.8 us (2%)
    pallas_call x1, Pallas kernels, shards(): pl.pallas_call(functools.partial(kernel, count), out_shape=jax.ShapeDtype...  345 us

profile of v4, /device:TPU:1, one launch (start us, length us, event | category | flops | bytes accessed | tf_op | source)
XLA Modules:
  0.0 355.4 jit_solution(136274484867451811)
XLA Ops:
  0.0 0.7 and_select_fusion
  0.7 0.5 pad_bitcast_fusion
  1.2 0.7 add_select_fusion
  1.9 0.0 copy-start
  1.9 0.8 copy.22
  2.7 0.7 multiply_bitcast_fusion
  3.4 0.6 pad.17.shot_amounts
  4.0 0.7 copy.26.shot_level
  4.7 1.0 copy.25.rec_level
  5.8 1.0 copy.24.rec_column
  6.8 1.0 copy.23
  7.8 0.8 pad.18.observed
  8.6 0.0 copy-done
  8.6 344.5 %shard_map.118 = f32[16,64,256]{2,1,0:T(8,128)} custom-call(f32[16,128,256]{2,1,0:T(8,128)} %coef_in.1, f32[16,128,256]{2,1,0:T(8,128)} %bitcast.17, f32[16,128,256]{2,1,0:T(8,128)} %bitcast.18, f32[16,128,256]{2,1,0:T(8,128)} %bitcast.19, f32[16,128,256]{2,1,0:T(8,128)} %bitcast.20, bf16[256,256]{1,0:T(8,128)(2,1)} %constant.126.clone.band, ...), custom_call_target="tpu_custom_call" | custom-call | tf_op jit(solution)/shard_map/pallas_call | solution.py:494
  353.1 2.3 copy.28
Async XLA Ops:
  1.9 6.8 %copy-start = (s32[1024]{0:T(1024)}, s32[1024]{0:T(1024)S(1)}, u32[]{:S(2)}) copy-start(s32[1024]{0:T(1024)S(1)} %get-tuple-element.6) | copy-start | bytes 12292
